TPU v7x, 512 devices: a whole 4x8x8 slice. The times are simulated.
512 devices in a mesh: slab: 64 (over x, z, core), head: 8 (over y).
Axes of the slice: x: 4, y: 8, z: 8, core: 2. Of those that a mesh axis runs over, the one named last changes fastest.
Arguments:
- queries: bfloat16 [16384, 4096], P('slab', 'head'), may hold values from -12 to 12, as said below
- keys: bfloat16 [16384, 2048], P('slab', 'head'), may hold values from -4 to 4
- values: bfloat16 [16384, 2048], P('slab', 'head'), may hold values from -5 to 5
- user_lengths: int32 [4], replicated, may hold values from 1 to 8192, 16384 in all
- page_slot: int32 [1024], replicated, may hold values from 0 to 1023, as said below
Outputs:
- attention_out: bfloat16 [16384, 4096], P(('slab', 'head'))
- kv_cache: bfloat16 [1024, 2, 16, 2048], P('slab', None, None, 'head')
Inputs may be any that keep to these rules, and one draw needn't show every extreme that they name: `queries`: entries are shaped as normal activations; the ends of the range are reached only by a few rows. `user_lengths`: every history has at least one token, they sum to 16384, and the longest has exactly 8192. `page_slot`: A permutation of the 1024 slots; slot s is held by slab index s // 16. The 16 pages of one slab go to 16 different slab indices, one slot each.
All inputs are finite; a program needn't handle non-finite values.
Results may differ from a plain program's by a relative error of at most 0.0042.
Values may be sent and summed in bfloat16 or wider, within the bound.
No kernel may reach another device: no remote copies, remote signals or barrier semaphores. Data moves between devices by JAX's collectives and lax.ppermute only.
A program may use at most 64 MiB of HBM per device.

v0:
```python
import jax
import jax.numpy as jnp
from jax import lax
from jax.sharding import PartitionSpec as P

HEAD_DIM = 128
WINDOW = 1024
PAGE_ROWS = 16


QUERY_SCALE = 168.0 ** (-0.5)
MASKED = -1e30


def shifted_2(block, axis, distance):
    devices = range(lax.axis_size(axis))
    route = [(i - distance, i) for i in devices if i - distance in devices]
    return lax.ppermute(block, axis, route)


def bounds(positions, user_lengths):
    user_ends = jnp.cumsum(user_lengths)
    user_starts = user_ends - user_lengths
    user_first = jnp.max(
        jnp.where(user_starts[None, :] <= positions[:, None], user_starts[None, :], 0), axis=1
    )
    user_last = jnp.min(
        jnp.where(user_ends[None, :] > positions[:, None], user_ends[None, :], user_ends[-1]),
        axis=1,
    )
    return (user_first, user_last)


def attend(query_rows, key_rows, value_rows, query_pos, key_pos, query_first):
    row_count = query_rows.shape[0]
    kv_local = key_rows.shape[1] // HEAD_DIM
    group_size = query_rows.shape[1] // (kv_local * HEAD_DIM)
    query_heads = query_rows.reshape(row_count, kv_local, group_size, HEAD_DIM)
    key_heads = key_rows.reshape(-1, kv_local, HEAD_DIM)
    value_heads = value_rows.reshape(-1, kv_local, HEAD_DIM)
    scores = (
        jnp.einsum("qgrd,kgd->grqk", query_heads, key_heads, preferred_element_type=jnp.float32)
        * QUERY_SCALE
    )
    allowed = (
        (key_pos[None, :] >= query_first[:, None])
        & (key_pos[None, :] <= query_pos[:, None])
        & (query_pos[:, None] - key_pos[None, :] < WINDOW)
    )
    scores = jnp.where(allowed[None, None], scores, MASKED)
    row_max = jnp.max(scores, axis=-1, keepdims=True)
    shifted = jnp.where(allowed[None, None], jnp.exp(scores - row_max), 0.0)
    denominators = jnp.sum(shifted, axis=-1)
    weights = shifted.astype(jnp.bfloat16)
    mixed = (
        jnp.einsum("grqk,kgd->grqd", weights, value_heads, preferred_element_type=jnp.float32)
        / denominators[..., None]
    )
    return (
        jnp.transpose(mixed, (2, 0, 1, 3))
        .reshape(row_count, query_rows.shape[1])
        .astype(jnp.bfloat16)
    )


def attend_slab(queries, keys, values, user_lengths, slab_first):
    tok_rows = queries.shape[0]
    reach = max(1, WINDOW // tok_rows)
    key_parts = []
    value_parts = []
    for shift_by in range(reach, 0, -1):
        moved = shifted_2((keys, values), "slab", shift_by)
        key_parts.append(moved[0])
        value_parts.append(moved[1])
    context_keys = jnp.concatenate(key_parts + [keys], axis=0)
    context_values = jnp.concatenate(value_parts + [values], axis=0)
    context_first = slab_first - reach * tok_rows
    block_rows = min(512, tok_rows)
    local_start = reach * tok_rows - WINDOW
    key_pos = context_first + local_start + jnp.arange(WINDOW + block_rows, dtype=jnp.int32)
    block_first = slab_first + 0
    query_pos = block_first + jnp.arange(block_rows, dtype=jnp.int32)
    query_first, unused_last = bounds(query_pos, user_lengths)
    result = attend(queries, context_keys, context_values, query_pos, key_pos, query_first)
    return result


def move_pages(keys, values, user_lengths, page_slot, slab_index, slab_first):
    tok_rows = keys.shape[0]
    kv_width = keys.shape[1]
    page_count = tok_rows // PAGE_ROWS
    slab_count = page_slot.shape[0] // page_count
    capacity = max(1, page_count // slab_count)
    own_positions = slab_first + jnp.arange(tok_rows, dtype=jnp.int32)
    unused_first, user_last = bounds(own_positions, user_lengths)
    live = own_positions >= user_last - WINDOW
    key_pages = jnp.where(live[:, None], keys, jnp.zeros_like(keys)).reshape(
        page_count, PAGE_ROWS, kv_width
    )
    value_pages = jnp.where(live[:, None], values, jnp.zeros_like(values)).reshape(
        page_count, PAGE_ROWS, kv_width
    )
    page_data = jnp.stack([key_pages, value_pages], axis=1)
    table = page_slot.reshape(slab_count, page_count)
    owners = table // page_count
    slots = table % page_count
    local_index = jnp.arange(page_count, dtype=jnp.int32)
    earlier = local_index[None, :] < local_index[:, None]
    same_owner = owners[:, :, None] == owners[:, None, :]
    ranks = jnp.sum(same_owner & earlier[None], axis=2)
    my_owners = lax.dynamic_index_in_dim(owners, slab_index, 0, keepdims=False)
    my_ranks = lax.dynamic_index_in_dim(ranks, slab_index, 0, keepdims=False)
    outgoing = jnp.zeros((slab_count, capacity, 2, PAGE_ROWS, kv_width), jnp.bfloat16)
    outgoing = outgoing.at[my_owners, my_ranks].set(page_data)
    incoming = lax.all_to_all(outgoing, "slab", split_axis=0, concat_axis=0, tiled=True)
    incoming = incoming.reshape(slab_count * capacity, 2, PAGE_ROWS, kv_width)
    mine = owners == slab_index
    targets = jnp.where(mine, slots, page_count).reshape(-1)
    sources = (jnp.arange(slab_count, dtype=jnp.int32)[:, None] * capacity + ranks).reshape(-1)
    source_of_slot = jnp.zeros((page_count,), jnp.int32).at[targets].set(sources, mode="drop")
    return incoming[source_of_slot]


def body(queries, keys, values, user_lengths, page_slot):
    slab_index = lax.axis_index("slab")
    slab_first = slab_index * queries.shape[0]
    attended = attend_slab(queries, keys, values, user_lengths, slab_first)
    kv_cache = move_pages(keys, values, user_lengths, page_slot, slab_index, slab_first)
    attention_out = lax.all_to_all(attended, "head", split_axis=0, concat_axis=1, tiled=True)
    return (attention_out, kv_cache)


def solution(mesh):
    return jax.shard_map(
        body,
        mesh=mesh,
        in_specs=(P("slab", "head"), P("slab", "head"), P("slab", "head"), P(), P()),
        out_specs=(P(("slab", "head"), None), P("slab", None, None, "head")),
        check_vma=False,
    )
```

profile of v0, /device:TPU:1, one launch (start us, length us, event | category | flops | bytes accessed | tf_op | source)
XLA Modules:
  0.0 107.3 jit_solution(2290993415051421893)
XLA Ops:
  0.6 0.0 copy-start
  0.6 1.0 copy.92
  1.7 6.6 %collective-permute-start.4 = (bf16[256,256]{0,1:T(8,128)(2,1)S(1)}, bf16[256,256]{0,1:T(8,128)(2,1)S(1)}, u32[]{:S(2)}, u32[]{:S(2)}) collective-permute-start(bf16[256,256]{0,1:T(8,128)(2,1)S(1)} %copy.92), channel_id=1, source_target_pairs={{0,32},{8,40},{16,48},{24,56},{32,64},{40,72},{48,80},{56,88},{64,... | collective-permute-start | bytes 393224 | tf_op jit(solution)/shard_map/ppermute | solution.py:18
  8.3 7.9 %collective-permute-start.5 = (bf16[256,256]{0,1:T(8,128)(2,1)S(1)}, bf16[256,256]{0,1:T(8,128)(2,1)S(1)}, u32[]{:S(2)}, u32[]{:S(2)}) collective-permute-start(bf16[256,256]{0,1:T(8,128)(2,1)S(1)} %copy.92), channel_id=1, source_target_pairs={{0,24},{8,32},{16,40},{24,48},{32,56},{40,64},{48,72},{56,80},{64,... | collective-permute-start | bytes 393224 | tf_op jit(solution)/shard_map/ppermute | solution.py:18
  16.2 3.1 %collective-permute-start.6 = (bf16[256,256]{0,1:T(8,128)(2,1)S(1)}, bf16[256,256]{0,1:T(8,128)(2,1)S(1)}, u32[]{:S(2)}, u32[]{:S(2)}) collective-permute-start(bf16[256,256]{0,1:T(8,128)(2,1)S(1)} %copy.92), channel_id=1, source_target_pairs={{0,16},{8,24},{16,32},{24,40},{32,48},{40,56},{48,64},{56,72},{64,... | collective-permute-start | bytes 393224 | tf_op jit(solution)/shard_map/ppermute | solution.py:18
  19.3 1.9 %collective-permute-start.7 = (bf16[256,256]{0,1:T(8,128)(2,1)S(1)}, bf16[256,256]{0,1:T(8,128)(2,1)S(1)}, u32[]{:S(2)}, u32[]{:S(2)}) collective-permute-start(bf16[256,256]{0,1:T(8,128)(2,1)S(1)} %copy.92), channel_id=1, source_target_pairs={{0,8},{8,16},{16,24},{24,32},{32,40},{40,48},{48,56},{56,64},{64,7... | collective-permute-start | bytes 393224 | tf_op jit(solution)/shard_map/ppermute | solution.py:18
  21.2 1.0 copy.85
  22.3 4.0 %collective-permute-start = (bf16[256,256]{0,1:T(8,128)(2,1)S(1)}, bf16[256,256]{0,1:T(8,128)(2,1)S(1)}, u32[]{:S(2)}, u32[]{:S(2)}) collective-permute-start(bf16[256,256]{0,1:T(8,128)(2,1)S(1)} %copy.85), channel_id=1, source_target_pairs={{0,32},{8,40},{16,48},{24,56},{32,64},{40,72},{48,80},{56,88},{64,... | collective-permute-start | bytes 393224 | tf_op jit(solution)/shard_map/ppermute | solution.py:18
  26.3 0.8 reduce-window.4
  27.1 0.6 slice.4
  27.7 0.7 bitcast_subtract_fusion
  28.4 0.8 reshape.269
  29.1 0.7 select_reduce_fusion
  29.9 1.1 broadcast_select_fusion.1
  30.9 0.4 fusion.8
  31.4 0.0 copy-done
  31.5 0.1 reshape.267
  31.5 0.1 copy.101
  31.6 0.0 collective-permute-done.4
  31.6 2.5 %collective-permute-start.1 = (bf16[256,256]{0,1:T(8,128)(2,1)S(1)}, bf16[256,256]{0,1:T(8,128)(2,1)S(1)}, u32[]{:S(2)}, u32[]{:S(2)}) collective-permute-start(bf16[256,256]{0,1:T(8,128)(2,1)S(1)} %copy.85), channel_id=1, source_target_pairs={{0,24},{8,32},{16,40},{24,48},{32,56},{40,64},{48,72},{56,80},{64,... | collective-permute-start | bytes 393224 | tf_op jit(solution)/shard_map/ppermute | solution.py:18
  34.1 0.0 collective-permute-done.5
  34.1 1.9 %collective-permute-start.2 = (bf16[256,256]{0,1:T(8,128)(2,1)S(1)}, bf16[256,256]{0,1:T(8,128)(2,1)S(1)}, u32[]{:S(2)}, u32[]{:S(2)}) collective-permute-start(bf16[256,256]{0,1:T(8,128)(2,1)S(1)} %copy.85), channel_id=1, source_target_pairs={{0,16},{8,24},{16,32},{24,40},{32,48},{40,56},{48,64},{56,72},{64,... | collective-permute-start | bytes 393224 | tf_op jit(solution)/shard_map/ppermute | solution.py:18
  36.1 0.0 collective-permute-done.6
  36.1 2.7 %collective-permute-start.3 = (bf16[256,256]{0,1:T(8,128)(2,1)S(1)}, bf16[256,256]{0,1:T(8,128)(2,1)S(1)}, u32[]{:S(2)}, u32[]{:S(2)}) collective-permute-start(bf16[256,256]{0,1:T(8,128)(2,1)S(1)} %copy.85), channel_id=1, source_target_pairs={{0,8},{8,16},{16,24},{24,32},{32,40},{40,48},{48,56},{56,64},{64,7... | collective-permute-start | bytes 393224 | tf_op jit(solution)/shard_map/ppermute | solution.py:18
  38.8 0.0 collective-permute-done.7
  38.9 0.0 collective-permute-done
  38.9 0.0 collective-permute-done.1
  38.9 1.6 %collective-permute-done.2 = bf16[256,256]{0,1:T(8,128)(2,1)S(1)} collective-permute-done((bf16[256,256]{0,1:T(8,128)(2,1)S(1)}, bf16[256,256]{0,1:T(8,128)(2,1)S(1)}, u32[]{:S(2)}, u32[]{:S(2)}) %collective-permute-start.2) | collective-permute-done | bytes 131104 | tf_op jit(solution)/shard_map/ppermute | solution.py:18
  40.6 2.4 %collective-permute-done.3 = bf16[256,256]{0,1:T(8,128)(2,1)S(1)} collective-permute-done((bf16[256,256]{0,1:T(8,128)(2,1)S(1)}, bf16[256,256]{0,1:T(8,128)(2,1)S(1)}, u32[]{:S(2)}, u32[]{:S(2)}) %collective-permute-start.3) | collective-permute-done | bytes 131104 | tf_op jit(solution)/shard_map/ppermute | solution.py:18
  43.0 2.5 %fusion.2 = f32[2,2,256]{2,1,0:T(2,128)S(1)} fusion(pred[256,1280]{0,1:T(8,128)(4,1)S(1)} %fusion.8, bf16[1280,2,128,1]{0,2,3,1:T(8,128)(2,1)S(1)} %bitcast.65, bf16[256,2,2,128]{3,2,1,0:T(2,128)(2,1)S(1)} %reshape.267), kind=kOutput, calls=%fused_computation.7 | convolution fusion | flops 342099200 | bytes 1249280 | tf_op jit(solution)/shard_map/sub | solution.py:52
  45.5 3.2 %fusion.15 = bf16[256,2,2,128]{3,0,2,1:T(8,128)(2,1)S(1)} fusion(bf16[1280,2,128,1]{0,2,3,1:T(8,128)(2,1)S(1)} %bitcast.64, pred[256,1280]{0,1:T(8,128)(4,1)S(1)} %fusion.8, bf16[1280,2,128,1]{0,2,3,1:T(8,128)(2,1)S(1)} %bitcast.66, f32[256,2,2]{0,2,1:T(2,128)S(1)} %bitcast.69, bf16[256,2,2,128]{3,2,1,0:T(2,128)(2,1)S(1)} %reshape.267), kind=kOutput, calls=%fused_computation.16 | convolution fusion | flops 677906688 | bytes 2166784 | tf_op jit(solution)/shard_map/grqk,kgd->grqd/dot_general | solution.py:56
  48.7 0.3 copy.99
  49.0 0.8 convert_element_type.15
  49.8 6.8 %all-to-all-start = ((bf16[8,32,512]{2,1,0:T(8,128)(2,1)}), bf16[8,32,512]{2,1,0:T(8,128)(2,1)S(1)}, u32[]{:S(2)}, u32[]{:S(2)}) async-start(bf16[8,32,512]{2,1,0:T(8,128)(2,1)} %convert_element_type.15), calls=%async_computation | async-start | bytes 524288 | tf_op jit(solution)/shard_map/all_to_all | solution.py:129
  56.6 0.1 convert_reduce_fusion
  56.8 0.2 dynamic-slice_reduce_fusion
  57.0 1.1 %broadcast.224 = bf16[64,2,16,256]{3,2,1,0:T(8,128)(2,1)} broadcast(bf16[]{:T(256)} %constant.67.clone.1), dimensions={} | broadcast | bytes 1048578 | tf_op jit(solution)/shard_map/broadcast_in_dim | solution.py:113
  58.1 2.5 %scatter_fusion = bf16[64,2,16,256]{3,2,1,0:T(8,128)(2,1)} fusion(bf16[64,2,16,256]{3,2,1,0:T(8,128)(2,1)} %broadcast.224, s32[16]{0:T(128)S(1)} %fusion.34, bf16[16,2,16,256]{3,2,1,0:T(8,128)(2,1)S(1)} %pad_maximum_fusion), kind=kCustom, calls=%fused_computation.1 | custom fusion | bytes 786496 | tf_op jit(solution)/shard_map/scatter | solution.py:114
  60.6 8.5 %all-to-all-done = bf16[8,32,512]{2,1,0:T(8,128)(2,1)S(1)} async-done(((bf16[8,32,512]{2,1,0:T(8,128)(2,1)}), bf16[8,32,512]{2,1,0:T(8,128)(2,1)S(1)}, u32[]{:S(2)}, u32[]{:S(2)}) %all-to-all-start) | async-done | bytes 262176 | tf_op jit(solution)/shard_map/all_to_all | solution.py:129
  69.1 0.0 copy-start.1
  69.1 8.4 %all-to-all-start.1 = ((bf16[64,1,2,16,256]{4,3,2,1,0:T(8,128)(2,1)}), bf16[64,1,2,16,256]{4,3,2,1,0:T(8,128)(2,1)S(1)}, u32[]{:S(2)}, u32[]{:S(2)}) async-start(bf16[64,1,2,16,256]{4,3,2,1,0:T(8,128)(2,1)} %bitcast.18), calls=%async_computation.1 | async-start | bytes 2097152 | tf_op jit(solution)/shard_map/all_to_all | solution.py:115
  77.5 0.1 copy.106
  77.6 0.1 reshape.293
  77.7 0.0 copy-done.1
  77.7 4.3 %scatter_custom_fusion.1 = s32[16]{0:T(128)S(1)} fusion(s32[1024]{0:T(1024)S(1)} %compare_select_fusion, s32[1024]{0:T(1024)S(1)} %reshape.293, s32[]{:T(128)} %constant.60.clone.1), kind=kCustom, calls=%fused_computation.68 | custom fusion | bytes 68 | tf_op jit(solution)/shard_map/scatter | solution.py:120
  82.0 0.7 copy.114
  82.7 23.3 %all-to-all-done.1 = bf16[64,1,2,16,256]{4,3,2,1,0:T(8,128)(2,1)S(1)} async-done(((bf16[64,1,2,16,256]{4,3,2,1,0:T(8,128)(2,1)}), bf16[64,1,2,16,256]{4,3,2,1,0:T(8,128)(2,1)S(1)}, u32[]{:S(2)}, u32[]{:S(2)}) %all-to-all-start.1) | async-done | bytes 1048608 | tf_op jit(solution)/shard_map/all_to_all | solution.py:115
  106.0 1.3 %gather_fusion = bf16[16,2,16,256]{3,2,1,0:T(8,128)(2,1)} fusion(bf16[64,2,16,256]{3,2,1,0:T(8,128)(2,1)S(1)} %bitcast.59, s32[1024]{0:T(1024)S(1)} %pad_clamp_fusion), kind=kCustom, calls=%fused_computation | custom fusion | bytes 524352 | tf_op jit(solution)/shard_map/gather | solution.py:121
  (21 shorter events, 0.2 us)
Async XLA Ops:
  0.6 30.8 %copy-start = (bf16[256,512]{1,0:T(8,128)(2,1)S(1)}, bf16[256,512]{1,0:T(8,128)(2,1)}, u32[]{:S(2)}) copy-start(bf16[256,512]{1,0:T(8,128)(2,1)} %param.5) | copy-start | bytes 786436
  1.7 29.9 %collective-permute-start.4 = (bf16[256,256]{0,1:T(8,128)(2,1)S(1)}, bf16[256,256]{0,1:T(8,128)(2,1)S(1)}, u32[]{:S(2)}, u32[]{:S(2)}) collective-permute-start(bf16[256,256]{0,1:T(8,128)(2,1)S(1)} %copy.92), channel_id=1, source_target_pairs={{0,32},{8,40},{16,48},{24,56},{32,64},{40,72},{48,80},{56,88},{64,... | collective-permute-start | bytes 393224 | tf_op jit(solution)/shard_map/ppermute | solution.py:18
  8.3 25.8 %collective-permute-start.5 = (bf16[256,256]{0,1:T(8,128)(2,1)S(1)}, bf16[256,256]{0,1:T(8,128)(2,1)S(1)}, u32[]{:S(2)}, u32[]{:S(2)}) collective-permute-start(bf16[256,256]{0,1:T(8,128)(2,1)S(1)} %copy.92), channel_id=1, source_target_pairs={{0,24},{8,32},{16,40},{24,48},{32,56},{40,64},{48,72},{56,80},{64,... | collective-permute-start | bytes 393224 | tf_op jit(solution)/shard_map/ppermute | solution.py:18
  16.2 19.9 %collective-permute-start.6 = (bf16[256,256]{0,1:T(8,128)(2,1)S(1)}, bf16[256,256]{0,1:T(8,128)(2,1)S(1)}, u32[]{:S(2)}, u32[]{:S(2)}) collective-permute-start(bf16[256,256]{0,1:T(8,128)(2,1)S(1)} %copy.92), channel_id=1, source_target_pairs={{0,16},{8,24},{16,32},{24,40},{32,48},{40,56},{48,64},{56,72},{64,... | collective-permute-start | bytes 393224 | tf_op jit(solution)/shard_map/ppermute | solution.py:18
  19.3 19.5 %collective-permute-start.7 = (bf16[256,256]{0,1:T(8,128)(2,1)S(1)}, bf16[256,256]{0,1:T(8,128)(2,1)S(1)}, u32[]{:S(2)}, u32[]{:S(2)}) collective-permute-start(bf16[256,256]{0,1:T(8,128)(2,1)S(1)} %copy.92), channel_id=1, source_target_pairs={{0,8},{8,16},{16,24},{24,32},{32,40},{40,48},{48,56},{56,64},{64,7... | collective-permute-start | bytes 393224 | tf_op jit(solution)/shard_map/ppermute | solution.py:18
  22.3 16.6 %collective-permute-start = (bf16[256,256]{0,1:T(8,128)(2,1)S(1)}, bf16[256,256]{0,1:T(8,128)(2,1)S(1)}, u32[]{:S(2)}, u32[]{:S(2)}) collective-permute-start(bf16[256,256]{0,1:T(8,128)(2,1)S(1)} %copy.85), channel_id=1, source_target_pairs={{0,32},{8,40},{16,48},{24,56},{32,64},{40,72},{48,80},{56,88},{64,... | collective-permute-start | bytes 393224 | tf_op jit(solution)/shard_map/ppermute | solution.py:18
  31.6 7.3 %collective-permute-start.1 = (bf16[256,256]{0,1:T(8,128)(2,1)S(1)}, bf16[256,256]{0,1:T(8,128)(2,1)S(1)}, u32[]{:S(2)}, u32[]{:S(2)}) collective-permute-start(bf16[256,256]{0,1:T(8,128)(2,1)S(1)} %copy.85), channel_id=1, source_target_pairs={{0,24},{8,32},{16,40},{24,48},{32,56},{40,64},{48,72},{56,80},{64,... | collective-permute-start | bytes 393224 | tf_op jit(solution)/shard_map/ppermute | solution.py:18
  34.1 6.5 %collective-permute-start.2 = (bf16[256,256]{0,1:T(8,128)(2,1)S(1)}, bf16[256,256]{0,1:T(8,128)(2,1)S(1)}, u32[]{:S(2)}, u32[]{:S(2)}) collective-permute-start(bf16[256,256]{0,1:T(8,128)(2,1)S(1)} %copy.85), channel_id=1, source_target_pairs={{0,16},{8,24},{16,32},{24,40},{32,48},{40,56},{48,64},{56,72},{64,... | collective-permute-start | bytes 393224 | tf_op jit(solution)/shard_map/ppermute | solution.py:18
  36.1 6.9 %collective-permute-start.3 = (bf16[256,256]{0,1:T(8,128)(2,1)S(1)}, bf16[256,256]{0,1:T(8,128)(2,1)S(1)}, u32[]{:S(2)}, u32[]{:S(2)}) collective-permute-start(bf16[256,256]{0,1:T(8,128)(2,1)S(1)} %copy.85), channel_id=1, source_target_pairs={{0,8},{8,16},{16,24},{24,32},{32,40},{40,48},{48,56},{56,64},{64,7... | collective-permute-start | bytes 393224 | tf_op jit(solution)/shard_map/ppermute | solution.py:18
  49.8 19.3 %all-to-all-start = ((bf16[8,32,512]{2,1,0:T(8,128)(2,1)}), bf16[8,32,512]{2,1,0:T(8,128)(2,1)S(1)}, u32[]{:S(2)}, u32[]{:S(2)}) async-start(bf16[8,32,512]{2,1,0:T(8,128)(2,1)} %convert_element_type.15), calls=%async_computation | async-start | bytes 524288 | tf_op jit(solution)/shard_map/all_to_all | solution.py:129
  69.1 8.6 %copy-start.1 = (s32[1024]{0:T(1024)S(1)}, s32[1024]{0:T(1024)}, u32[]{:S(2)}) copy-start(s32[1024]{0:T(1024)} %param.9) | copy-start | bytes 12292
  69.1 37.0 %all-to-all-start.1 = ((bf16[64,1,2,16,256]{4,3,2,1,0:T(8,128)(2,1)}), bf16[64,1,2,16,256]{4,3,2,1,0:T(8,128)(2,1)S(1)}, u32[]{:S(2)}, u32[]{:S(2)}) async-start(bf16[64,1,2,16,256]{4,3,2,1,0:T(8,128)(2,1)} %bitcast.18), calls=%async_computation.1 | async-start | bytes 2097152 | tf_op jit(solution)/shard_map/all_to_all | solution.py:115
where the time goes:
time: 108 us; the launch traced here: 107 us
  starting transfers between devices  45.9 us (42%)
  waiting for transfers between devices  35.9 us (33%)
  local copies, waits for them, and re-layouts  14.9 us (14%)
  matrix products  5.7 us (5%)
  other arithmetic  3.96 us (4%)
    ppermute x8, starting transfers between devices, shifted_2(): return lax.ppermute(block, axis, route)  30.7 us
    all_to_all x1, waiting for transfers between devices, move_pages(): lax.all_to_all(outgoing, 'slab', split_axis=0, concat_axis=0, tiled=True)  23.3 us
    all_to_all x1, waiting for transfers between devices, body(): lax.all_to_all(attended, 'head', split_axis=0, concat_axis=1, tiled=True)  8.5 us
    all_to_all x1, starting transfers between devices, move_pages(): lax.all_to_all(outgoing, 'slab', split_axis=0, concat_axis=0, tiled=True)  8.41 us
    all_to_all x1, starting transfers between devices, body(): lax.all_to_all(attended, 'head', split_axis=0, concat_axis=1, tiled=True)  6.83 us
    scatter x1, local copies, waits for them, and re-layouts, move_pages(): jnp.zeros((page_count,), jnp.int32).at[targets].set(sources, mode='drop')  4.3 us
    ppermute x8, waiting for transfers between devices, shifted_2(): return lax.ppermute(block, axis, route)  4.05 us
    dot_general x1, matrix products, attend(): jnp.einsum('grqk,kgd->grqd', weights, value_heads, preferred_element_type...  3.19 us
  transfers between devices with their start and end apart: 10, of which 4 were waited for; matrix products, arithmetic and copies ran while one was open for 14% of the time, Pallas kernels for 0%

commit v1 on v0

v1 whole, which is shorter than its diff:
```python
import functools

import jax
import jax.numpy as jnp
from jax import lax
from jax.experimental import pallas as pl
from jax.experimental.pallas import tpu as pltpu
from jax.sharding import Mesh
from jax.sharding import PartitionSpec as P

HEAD_DIM = 128
WINDOW = 1024
PAGE_ROWS = 16
QUERY_SCALE = 168.0 ** (-0.5)
LOG2_E = 1.4426950408889634
MASKED = -1e30
CORES = 2
ATTEND_WEIGHT = 22

VMEM = pl.BlockSpec(memory_space=pltpu.VMEM)
SMEM = pl.BlockSpec(memory_space=pltpu.SMEM)
ANY = pl.BlockSpec(memory_space=pl.ANY)


def user_first(positions, lengths_ref):
    first = jnp.zeros_like(positions)
    start = jnp.int32(0)
    for user in range(lengths_ref.shape[0]):
        first = jnp.where(positions >= start, start, first)
        start = start + lengths_ref[user]
    return first


def user_last(positions, lengths_ref):
    ends = []
    end = jnp.int32(0)
    for user in range(lengths_ref.shape[0]):
        end = end + lengths_ref[user]
        ends.append(end)
    last = jnp.zeros_like(positions) + ends[-1]
    for end in reversed(ends[:-1]):
        last = jnp.where(positions < end, end, last)
    return last


def pages_kernel(place_ref, lengths_ref, slot_ref, own_ref, out_ref):
    slab = place_ref[0]
    tokens, kv_width = own_ref.shape[1:]
    pages = tokens // PAGE_ROWS
    out_ref[...] = jnp.zeros_like(out_ref)
    for page in range(pages):
        rows = slice(page * PAGE_ROWS, (page + 1) * PAGE_ROWS)
        positions = (slab * pages + page) * PAGE_ROWS + lax.broadcasted_iota(
            jnp.int32, (PAGE_ROWS, kv_width), 0
        )
        live = positions >= user_last(positions, lengths_ref) - WINDOW
        owner = slot_ref[slab * pages + page] // pages
        for side in range(2):
            out_ref[owner, side] = jnp.where(live, own_ref[side, rows, :], 0).astype(out_ref.dtype)


def collect_kernel(source_ref, in_ref, out_ref, sems):
    copies = [
        pltpu.make_async_copy(in_ref.at[source_ref[slot]], out_ref.at[slot], sems.at[slot])
        for slot in range(out_ref.shape[0])
    ]
    for copy in copies:
        copy.start()
    for copy in copies:
        copy.wait()


def attend_kernel(
    place_ref, lengths_ref, queries_ref, own_ref, near_ref, far_ref, partner_ref, out_ref
):
    slab, core = place_ref[0], place_ref[1]
    tokens = queries_ref.shape[0]
    kv_local = own_ref.shape[2] // HEAD_DIM
    group = queries_ref.shape[1] // (kv_local * HEAD_DIM)
    first_core = core == 0
    pieces = [
        (own_ref, 0),
        (near_ref, 2),
        (far_ref, 4),
        (partner_ref.at[0], jnp.where(first_core, 1, 3)),
        (partner_ref.at[1], jnp.where(first_core, 3, 1)),
    ]
    row = lax.broadcasted_iota(jnp.int32, (tokens, 1), 0)
    column = lax.broadcasted_iota(jnp.int32, (tokens, tokens), 1)
    first = user_first(slab * tokens + row, lengths_ref)
    causal = column <= lax.broadcasted_iota(jnp.int32, (tokens, tokens), 0)
    for g in range(kv_local):
        kv_columns = slice(g * HEAD_DIM, (g + 1) * HEAD_DIM)
        for r in range(group):
            h = g * group + r
            query = queries_ref[:, h * HEAD_DIM : (h + 1) * HEAD_DIM]
            scores = []
            for ref, back in pieces:
                s = lax.dot_general(
                    query,
                    ref[0, :, kv_columns],
                    (((1,), (1,)), ((), ())),
                    preferred_element_type=jnp.float32,
                )
                begin = first - (slab - back) * tokens
                if ref is far_ref:
                    begin = jnp.maximum(begin, row + 1)
                allowed = column >= begin
                if ref is own_ref:
                    allowed = allowed & causal
                scores.append(jnp.where(allowed, s, MASKED))
            peak = functools.reduce(jnp.maximum, scores)
            row_max = jnp.max(peak, axis=1, keepdims=True)
            total, mixed = None, None
            for (ref, back), s in zip(pieces, scores):
                shifted = jnp.exp2((s - row_max) * (QUERY_SCALE * LOG2_E))
                part = jnp.dot(
                    shifted.astype(jnp.bfloat16),
                    ref[1, :, kv_columns],
                    preferred_element_type=jnp.float32,
                )
                total = shifted if total is None else total + shifted
                mixed = part if mixed is None else mixed + part
            denominators = jnp.sum(total, axis=1, keepdims=True)
            out_ref[:, h * HEAD_DIM : (h + 1) * HEAD_DIM] = (mixed / denominators).astype(
                out_ref.dtype
            )


def cost(flops, moved):
    return pl.CostEstimate(flops=flops, bytes_accessed=moved, transcendentals=0)


def body(queries, keys, values, user_lengths, page_slot):
    slab_axes = ("x", "z", "core")
    tokens, kv_width = keys.shape
    slabs = page_slot.shape[0] // (tokens // PAGE_ROWS)
    pages = tokens // PAGE_ROWS
    slab = lax.axis_index(slab_axes)
    core = lax.axis_index("core")
    place = jnp.stack([slab, core]).astype(jnp.int32)

    own = jnp.stack([keys, values])
    outgoing = pl.pallas_call(
        pages_kernel,
        out_shape=jax.ShapeDtypeStruct((slabs, 2, PAGE_ROWS, kv_width), jnp.bfloat16),
        in_specs=[SMEM, SMEM, SMEM, VMEM],
        out_specs=VMEM,
        cost_estimate=cost(0, slabs * pages * PAGE_ROWS * kv_width * 4),
        name="pages",
    )(place, user_lengths, page_slot, own)
    incoming = lax.all_to_all(outgoing, slab_axes, split_axis=0, concat_axis=0, tiled=True)
    chips = lax.axis_size("x") * lax.axis_size("z")
    near, far = [
        lax.ppermute(own, ("x", "z"), [(i, i + hop) for i in range(chips - hop)])
        for hop in (1, 2)
    ]
    given = jnp.stack([near, jnp.where(core == 0, own, far)])
    partner = lax.ppermute(given, "core", [(0, 1), (1, 0)])

    slots = slab * pages + jnp.arange(pages, dtype=jnp.int32)
    page_index = jnp.arange(page_slot.shape[0], dtype=jnp.int32)
    source = jnp.sum(
        jnp.where(page_slot[None, :] == slots[:, None], page_index[None, :] // pages, 0), axis=1
    )

    attended = pl.pallas_call(
        attend_kernel,
        out_shape=jax.ShapeDtypeStruct(queries.shape, jnp.bfloat16),
        in_specs=[SMEM, SMEM, VMEM, VMEM, VMEM, VMEM, VMEM],
        out_specs=VMEM,
        cost_estimate=cost(ATTEND_WEIGHT * 4 * queries.shape[0] * queries.shape[1] * 5 * tokens, 2 << 20),
        compiler_params=pltpu.CompilerParams(vmem_limit_bytes=24 << 20),
        name="attend",
    )(place, user_lengths, queries, own, near, far, partner)
    attended, incoming = lax.optimization_barrier((attended, incoming))
    attention_out = lax.all_to_all(attended, "head", split_axis=0, concat_axis=1, tiled=True)

    kv_cache = pl.pallas_call(
        collect_kernel,
        out_shape=jax.ShapeDtypeStruct((pages, 2, PAGE_ROWS, kv_width), jnp.bfloat16),
        in_specs=[SMEM, ANY],
        out_specs=VMEM,
        scratch_shapes=[pltpu.SemaphoreType.DMA((pages,))],
        cost_estimate=cost(0, pages * PAGE_ROWS * kv_width * 8),
        name="collect",
    )(source, incoming)
    return attention_out, kv_cache


def solution(mesh):
    x, z, y = 4, 8, mesh.shape["head"]
    chips = mesh.shape["slab"] // CORES
    z = next(n for n in (8, 4, 2, 1) if chips % n == 0)
    x = chips // z
    split = Mesh(mesh.devices.reshape(x, z, CORES, y), ("x", "z", "core", "head"))
    return jax.shard_map(
        body,
        mesh=split,
        in_specs=(
            P(("x", "z", "core"), "head"),
            P(("x", "z", "core"), "head"),
            P(("x", "z", "core"), "head"),
            P(),
            P(),
        ),
        out_specs=(
            P(("x", "z", "core", "head"), None),
            P(("x", "z", "core"), None, None, "head"),
        ),
        check_vma=False,
    )
```

time: 108 us -> 75 us (0.69)
  the two profiles are of different devices: /device:TPU:1 before, /device:TPU:6 now
where the time goes in v1:
time: 75 us; the launch traced here: 73.7 us
  starting transfers between devices  30.9 us (41%)
  waiting for transfers between devices  29.7 us (40%)
  Pallas kernels  8.41 us (11%)
  other arithmetic  2.45 us (3%)
  local copies, waits for them, and re-layouts  1.41 us (2%)
  between operations  0.78 us (1%)
    all_to_all x1, waiting for transfers between devices, body(): lax.all_to_all(outgoing, slab_axes, split_axis=0, concat_axis=0, tiled=True)  15.6 us
    all_to_all x1, starting transfers between devices, body(): lax.all_to_all(outgoing, slab_axes, split_axis=0, concat_axis=0, tiled=True)  11.4 us
    ppermute x2, starting transfers between devices, body(): lax.ppermute(own, ('x', 'z'), [(i, i + hop) for i in range(chips - hop)])  10.4 us
    all_to_all x1, waiting for transfers between devices, body(): lax.all_to_all(attended, 'head', split_axis=0, concat_axis=1, tiled=True)  8 us
    all_to_all x1, starting transfers between devices, body(): lax.all_to_all(attended, 'head', split_axis=0, concat_axis=1, tiled=True)  7.1 us
    ppermute x2, waiting for transfers between devices, body(): lax.ppermute(own, ('x', 'z'), [(i, i + hop) for i in range(chips - hop)])  4.19 us
    pallas_call x1, Pallas kernels, body(): pl.pallas_call(attend_kernel, out_shape=jax.ShapeDtypeStruct(queries.shap...  3.95 us
    pallas_call x1, Pallas kernels, body(): pl.pallas_call(collect_kernel, out_shape=jax.ShapeDtypeStruct((pages, 2,...  2.4 us
  transfers between devices with their start and end apart: 5, of which 4 were waited for; matrix products, arithmetic and copies ran while one was open for 2% of the time, Pallas kernels for 11%

profile of v1, /device:TPU:6, one launch (start us, length us, event | category | flops | bytes accessed | tf_op | source)
XLA Modules:
  0.0 73.7 jit_solution(14966757994606643585)
XLA Ops:
  0.6 1.0 %pad_maximum_fusion.1.own_ref = bf16[2,256,256]{2,1,0:T(8,128)(2,1)S(1)} fusion(bf16[1,256,256]{2,1,0:T(8,128)(2,1)} %bitcast.13, bf16[1,256,256]{2,1,0:T(8,128)(2,1)} %bitcast.15), kind=kLoop, calls=%fused_computation.1 | loop fusion | flops 131072 | bytes 524288 | tf_op jit(solution)/shard_map/stack | solution.py:143
  1.6 0.0 copy-start
  1.6 6.1 %collective-permute-start.1 = (bf16[2,256,256]{2,1,0:T(8,128)(2,1)S(1)}, bf16[2,256,256]{2,1,0:T(8,128)(2,1)S(1)}, u32[]{:S(2)}, u32[]{:S(2)}) collective-permute-start(bf16[2,256,256]{2,1,0:T(8,128)(2,1)S(1)} %pad_maximum_fusion.1.own_ref), channel_id=1, source_target_pairs={{0,32},{16,48},{32,64},{48,80},{64,96},{80,112},{96,128},{112,144}... | collective-permute-start | bytes 786440 | tf_op jit(solution)/shard_map/ppermute | solution.py:155
  7.7 4.3 %collective-permute-start = (bf16[2,256,256]{2,1,0:T(8,128)(2,1)S(1)}, bf16[2,256,256]{2,1,0:T(8,128)(2,1)S(1)}, u32[]{:S(2)}, u32[]{:S(2)}) collective-permute-start(bf16[2,256,256]{2,1,0:T(8,128)(2,1)S(1)} %pad_maximum_fusion.1.own_ref), channel_id=1, source_target_pairs={{0,16},{16,32},{32,48},{48,64},{64,80},{80,96},{96,112},{112,128},... | collective-permute-start | bytes 786440 | tf_op jit(solution)/shard_map/ppermute | solution.py:155
  12.0 0.7 pad_add_fusion.place_ref
  12.7 0.0 copy-done
  12.7 2.1 %pages.1 = bf16[64,2,16,256]{3,2,1,0:T(8,128)(2,1)} custom-call(s32[2]{0:T(128)} %pad_add_fusion.place_ref, s32[4]{0:T(128)} %lengths_ref.3, s32[1024]{0:T(1024)} %slot_ref.1, bf16[2,256,256]{2,1,0:T(8,128)(2,1)} %copy-done), custom_call_target="tpu_custom_call" | custom-call | bytes 16777216 | tf_op jit(solution)/shard_map/pages/pallas_call | solution.py:144
  14.8 0.0 copy-start.6
  14.8 0.0 copy-start.7
  14.8 11.4 %all-to-all-start = ((bf16[64,2,16,256]{3,2,1,0:T(8,128)(2,1)}), bf16[64,2,16,256]{3,2,1,0:T(8,128)(2,1)S(1)}, u32[]{:S(2)}, u32[]{:S(2)}) async-start(bf16[64,2,16,256]{3,2,1,0:T(8,128)(2,1)} %pages.1), calls=%async_computation | async-start | bytes 2097152 | tf_op jit(solution)/shard_map/all_to_all | solution.py:152
  26.2 0.0 collective-permute-done.1.far_ref
  26.2 0.0 copy-done.6
  26.2 0.0 copy-done.7
  26.3 4.2 %collective-permute-done.near_ref = bf16[2,256,256]{2,1,0:T(8,128)(2,1)S(1)} collective-permute-done((bf16[2,256,256]{2,1,0:T(8,128)(2,1)S(1)}, bf16[2,256,256]{2,1,0:T(8,128)(2,1)S(1)}, u32[]{:S(2)}, u32[]{:S(2)}) %collective-permute-start) | collective-permute-done | bytes 262176 | tf_op jit(solution)/shard_map/ppermute | solution.py:155
  30.5 0.0 copy-start.1
  30.5 0.0 copy-start.2
  30.5 0.0 copy-start.3
  30.5 0.0 copy-start.4
  30.5 0.1 pad_maximum_fusion
  30.5 2.1 %collective-permute-start.2 = (bf16[2,2,256,256]{3,2,1,0:T(8,128)(2,1)S(1)}, bf16[2,2,256,256]{3,2,1,0:T(8,128)(2,1)S(1)}, u32[]{:S(2)}, u32[]{:S(2)}) collective-permute-start(bf16[2,2,256,256]{3,2,1,0:T(8,128)(2,1)S(1)} %pad_maximum_fusion), channel_id=1, source_target_pairs={{0,8},{8,0},{1,9},{9,1},{2,10},{10,2},{3,11},{11,3},{4,12},{12,4},... | collective-permute-start | bytes 1572872 | tf_op jit(solution)/shard_map/ppermute | solution.py:159
  32.6 1.9 %collective-permute-done.2.partner_ref = bf16[2,2,256,256]{3,2,1,0:T(8,128)(2,1)S(1)} collective-permute-done((bf16[2,2,256,256]{3,2,1,0:T(8,128)(2,1)S(1)}, bf16[2,2,256,256]{3,2,1,0:T(8,128)(2,1)S(1)}, u32[]{:S(2)}, u32[]{:S(2)}) %collective-permute-start.2) | collective-permute-done | bytes 524320 | tf_op jit(solution)/shard_map/ppermute | solution.py:159
  34.5 0.0 copy-done.1
  34.5 0.0 copy-done.2
  34.5 0.0 copy-done.3
  34.5 0.0 copy-done.4
  34.5 4.0 %attend.1 = bf16[256,512]{1,0:T(8,128)(2,1)} custom-call(s32[2]{0:T(128)S(1)} %copy-done.3, s32[4]{0:T(128)S(1)} %copy-done.2, bf16[256,512]{1,0:T(8,128)(2,1)S(1)} %copy-done.4, bf16[2,256,256]{2,1,0:T(8,128)(2,1)S(1)} %copy-done.1, bf16[2,256,256]{2,1,0:T(8,128)(2,1)S(1)} %collective-permute-done.near_ref, ...), custom_call_target="tpu_custom_call" | custom-call | flops 14763950080 | bytes 2097152 | tf_op jit(solution)/shard_map/attend/pallas_call | solution.py:167
  38.5 15.6 %all-to-all-done.in_ref = bf16[64,2,16,256]{3,2,1,0:T(8,128)(2,1)S(1)} async-done(((bf16[64,2,16,256]{3,2,1,0:T(8,128)(2,1)}), bf16[64,2,16,256]{3,2,1,0:T(8,128)(2,1)S(1)}, u32[]{:S(2)}, u32[]{:S(2)}) %all-to-all-start) | async-done | bytes 1048608 | tf_op jit(solution)/shard_map/all_to_all | solution.py:152
  54.0 0.0 copy-start.5
  54.1 7.1 %all-to-all-start.1 = ((bf16[8,32,512]{2,1,0:T(8,128)(2,1)}), bf16[8,32,512]{2,1,0:T(8,128)(2,1)S(1)}, u32[]{:S(2)}, u32[]{:S(2)}) async-start(bf16[8,32,512]{2,1,0:T(8,128)(2,1)} %bitcast.6), calls=%async_computation.1 | async-start | bytes 524288 | tf_op jit(solution)/shard_map/all_to_all | solution.py:177
  61.2 0.0 copy-start.8
  61.2 0.7 copy-done.8
  61.8 0.7 select_reduce_fusion.source_ref
  62.5 0.0 copy-done.5
  62.5 2.4 %collect.1 = bf16[16,2,16,256]{3,2,1,0:T(8,128)(2,1)} custom-call(s32[16]{0:T(128)} %select_reduce_fusion.source_ref, bf16[64,2,16,256]{3,2,1,0:T(8,128)(2,1)} %copy-done.5), custom_call_target="tpu_custom_call" | custom-call | bytes 524288 | tf_op jit(solution)/shard_map/collect/pallas_call | solution.py:179
  64.9 8.0 %all-to-all-done.1 = bf16[8,32,512]{2,1,0:T(8,128)(2,1)S(1)} async-done(((bf16[8,32,512]{2,1,0:T(8,128)(2,1)}), bf16[8,32,512]{2,1,0:T(8,128)(2,1)S(1)}, u32[]{:S(2)}, u32[]{:S(2)}) %all-to-all-start.1) | async-done | bytes 262176 | tf_op jit(solution)/shard_map/all_to_all | solution.py:177
  72.9 0.7 copy.9
  (3 shorter events, 0.0 us)
Async XLA Ops:
  1.6 11.1 %copy-start = (bf16[2,256,256]{2,1,0:T(8,128)(2,1)}, bf16[2,256,256]{2,1,0:T(8,128)(2,1)S(1)}, u32[]{:S(2)}) copy-start(bf16[2,256,256]{2,1,0:T(8,128)(2,1)S(1)} %pad_maximum_fusion.1.own_ref) | copy-start | bytes 786436
  1.6 24.6 %collective-permute-start.1 = (bf16[2,256,256]{2,1,0:T(8,128)(2,1)S(1)}, bf16[2,256,256]{2,1,0:T(8,128)(2,1)S(1)}, u32[]{:S(2)}, u32[]{:S(2)}) collective-permute-start(bf16[2,256,256]{2,1,0:T(8,128)(2,1)S(1)} %pad_maximum_fusion.1.own_ref), channel_id=1, source_target_pairs={{0,32},{16,48},{32,64},{48,80},{64,96},{80,112},{96,128},{112,144}... | collective-permute-start | bytes 786440 | tf_op jit(solution)/shard_map/ppermute | solution.py:155
  7.7 22.7 %collective-permute-start = (bf16[2,256,256]{2,1,0:T(8,128)(2,1)S(1)}, bf16[2,256,256]{2,1,0:T(8,128)(2,1)S(1)}, u32[]{:S(2)}, u32[]{:S(2)}) collective-permute-start(bf16[2,256,256]{2,1,0:T(8,128)(2,1)S(1)} %pad_maximum_fusion.1.own_ref), channel_id=1, source_target_pairs={{0,16},{16,32},{32,48},{48,64},{64,80},{80,96},{96,112},{112,128},... | collective-permute-start | bytes 786440 | tf_op jit(solution)/shard_map/ppermute | solution.py:155
  14.8 11.5 %copy-start.6 = (bf16[256,256]{1,0:T(8,128)(2,1)S(1)}, bf16[256,256]{1,0:T(8,128)(2,1)}, u32[]{:S(2)}) copy-start(bf16[256,256]{1,0:T(8,128)(2,1)} %param.7) | copy-start | bytes 393220
  14.8 11.5 %copy-start.7 = (bf16[256,256]{1,0:T(8,128)(2,1)S(1)}, bf16[256,256]{1,0:T(8,128)(2,1)}, u32[]{:S(2)}) copy-start(bf16[256,256]{1,0:T(8,128)(2,1)} %param.6) | copy-start | bytes 393220
  14.8 39.3 %all-to-all-start = ((bf16[64,2,16,256]{3,2,1,0:T(8,128)(2,1)}), bf16[64,2,16,256]{3,2,1,0:T(8,128)(2,1)S(1)}, u32[]{:S(2)}, u32[]{:S(2)}) async-start(bf16[64,2,16,256]{3,2,1,0:T(8,128)(2,1)} %pages.1), calls=%async_computation | async-start | bytes 2097152 | tf_op jit(solution)/shard_map/all_to_all | solution.py:152
  30.5 4.0 %copy-start.1 = (bf16[2,256,256]{2,1,0:T(8,128)(2,1)S(1)}, bf16[2,256,256]{2,1,0:T(8,128)(2,1)}, u32[]{:S(2)}) copy-start(bf16[2,256,256]{2,1,0:T(8,128)(2,1)} %copy-done) | copy-start | bytes 786436
  30.5 4.0 %copy-start.2 = (s32[4]{0:T(128)S(1)}, s32[4]{0:T(128)}, u32[]{:S(2)}) copy-start(s32[4]{0:T(128)} %lengths_ref.3) | copy-start | bytes 52
  30.5 4.0 %copy-start.3 = (s32[2]{0:T(128)S(1)}, s32[2]{0:T(128)}, u32[]{:S(2)}) copy-start(s32[2]{0:T(128)} %pad_add_fusion.place_ref) | copy-start | bytes 28
  30.5 4.0 %copy-start.4 = (bf16[256,512]{1,0:T(8,128)(2,1)S(1)}, bf16[256,512]{1,0:T(8,128)(2,1)}, u32[]{:S(2)}) copy-start(bf16[256,512]{1,0:T(8,128)(2,1)} %queries_ref.1) | copy-start | bytes 786436
  30.5 3.9 %collective-permute-start.2 = (bf16[2,2,256,256]{3,2,1,0:T(8,128)(2,1)S(1)}, bf16[2,2,256,256]{3,2,1,0:T(8,128)(2,1)S(1)}, u32[]{:S(2)}, u32[]{:S(2)}) collective-permute-start(bf16[2,2,256,256]{3,2,1,0:T(8,128)(2,1)S(1)} %pad_maximum_fusion), channel_id=1, source_target_pairs={{0,8},{8,0},{1,9},{9,1},{2,10},{10,2},{3,11},{11,3},{4,12},{12,4},... | collective-permute-start | bytes 1572872 | tf_op jit(solution)/shard_map/ppermute | solution.py:159
  54.0 8.5 %copy-start.5 = (bf16[64,2,16,256]{3,2,1,0:T(8,128)(2,1)}, bf16[64,2,16,256]{3,2,1,0:T(8,128)(2,1)S(1)}, u32[]{:S(2)}) copy-start(bf16[64,2,16,256]{3,2,1,0:T(8,128)(2,1)S(1)} %all-to-all-done.in_ref) | copy-start | bytes 3145732
  54.1 18.9 %all-to-all-start.1 = ((bf16[8,32,512]{2,1,0:T(8,128)(2,1)}), bf16[8,32,512]{2,1,0:T(8,128)(2,1)S(1)}, u32[]{:S(2)}, u32[]{:S(2)}) async-start(bf16[8,32,512]{2,1,0:T(8,128)(2,1)} %bitcast.6), calls=%async_computation.1 | async-start | bytes 524288 | tf_op jit(solution)/shard_map/all_to_all | solution.py:177
  61.2 0.7 copy-start.8

commit v2 on v1

--- a/solution.py
+++ b/solution.py
@@ -15,7 +15,8 @@
 LOG2_E = 1.4426950408889634
 MASKED = -1e30
 CORES = 2
-ATTEND_WEIGHT = 22
+HALVES = 2
+ATTEND_WEIGHT = 14
 
 VMEM = pl.BlockSpec(memory_space=pltpu.VMEM)
 SMEM = pl.BlockSpec(memory_space=pltpu.SMEM)
@@ -43,41 +44,46 @@
     return last
 
 
-def pages_kernel(place_ref, lengths_ref, slot_ref, own_ref, out_ref):
-    slab = place_ref[0]
-    tokens, kv_width = own_ref.shape[1:]
+def here():
+    core = lax.axis_index("core")
+    chip = lax.axis_index("x") * lax.axis_size("z") + lax.axis_index("z")
+    return chip * CORES + core, core
+
+
+def prepare_kernel(lengths_ref, slot_ref, keys_ref, values_ref, out_ref, live_ref, sems):
+    slab, _ = here()
+    tokens, kv_width = keys_ref.shape
     pages = tokens // PAGE_ROWS
-    out_ref[...] = jnp.zeros_like(out_ref)
+    copies = []
     for page in range(pages):
         rows = slice(page * PAGE_ROWS, (page + 1) * PAGE_ROWS)
         positions = (slab * pages + page) * PAGE_ROWS + lax.broadcasted_iota(
             jnp.int32, (PAGE_ROWS, kv_width), 0
         )
         live = positions >= user_last(positions, lengths_ref) - WINDOW
+        for side, ref in enumerate((keys_ref, values_ref)):
+            live_ref[page, side] = jnp.where(live, ref[rows, :], 0).astype(live_ref.dtype)
         owner = slot_ref[slab * pages + page] // pages
-        for side in range(2):
-            out_ref[owner, side] = jnp.where(live, own_ref[side, rows, :], 0).astype(out_ref.dtype)
-
-
-def collect_kernel(source_ref, in_ref, out_ref, sems):
-    copies = [
-        pltpu.make_async_copy(in_ref.at[source_ref[slot]], out_ref.at[slot], sems.at[slot])
-        for slot in range(out_ref.shape[0])
-    ]
-    for copy in copies:
-        copy.start()
+        copies.append(pltpu.make_async_copy(live_ref.at[page], out_ref.at[owner], sems.at[page]))
+        copies[-1].start()
     for copy in copies:
         copy.wait()
 
 
+def collect_kernel(source_ref, in_ref, out_ref):
+    for slot in range(out_ref.shape[0]):
+        out_ref[slot] = in_ref[source_ref[slot]]
+
+
 def attend_kernel(
-    place_ref, lengths_ref, queries_ref, own_ref, near_ref, far_ref, partner_ref, out_ref
+    lengths_ref, queries_ref, own_ref, near_ref, far_ref, partner_ref, kept_ref, sent_ref
 ):
-    slab, core = place_ref[0], place_ref[1]
+    slab, core = here()
     tokens = queries_ref.shape[0]
     kv_local = own_ref.shape[2] // HEAD_DIM
     group = queries_ref.shape[1] // (kv_local * HEAD_DIM)
     first_core = core == 0
+    first_half = lax.axis_index("half") == 0
     pieces = [
         (own_ref, 0),
         (near_ref, 2),
@@ -122,9 +128,11 @@
                 total = shifted if total is None else total + shifted
                 mixed = part if mixed is None else mixed + part
             denominators = jnp.sum(total, axis=1, keepdims=True)
-            out_ref[:, h * HEAD_DIM : (h + 1) * HEAD_DIM] = (mixed / denominators).astype(
-                out_ref.dtype
-            )
+            result = (mixed / denominators).astype(kept_ref.dtype)
+            lower, upper = result[: tokens // HALVES], result[tokens // HALVES :]
+            columns = slice(h * HEAD_DIM, (h + 1) * HEAD_DIM)
+            kept_ref[:, columns] = jnp.where(first_half, lower, upper)
+            sent_ref[:, columns] = jnp.where(first_half, upper, lower)
 
 
 def cost(flops, moved):
@@ -138,17 +146,21 @@
     pages = tokens // PAGE_ROWS
     slab = lax.axis_index(slab_axes)
     core = lax.axis_index("core")
-    place = jnp.stack([slab, core]).astype(jnp.int32)
-
+
+    page_block = (2, PAGE_ROWS, kv_width)
     own = jnp.stack([keys, values])
     outgoing = pl.pallas_call(
-        pages_kernel,
-        out_shape=jax.ShapeDtypeStruct((slabs, 2, PAGE_ROWS, kv_width), jnp.bfloat16),
-        in_specs=[SMEM, SMEM, SMEM, VMEM],
-        out_specs=VMEM,
-        cost_estimate=cost(0, slabs * pages * PAGE_ROWS * kv_width * 4),
-        name="pages",
-    )(place, user_lengths, page_slot, own)
+        prepare_kernel,
+        out_shape=jax.ShapeDtypeStruct((slabs,) + page_block, jnp.bfloat16),
+        in_specs=[SMEM, SMEM, VMEM, VMEM],
+        out_specs=ANY,
+        scratch_shapes=[
+            pltpu.VMEM((pages,) + page_block, jnp.bfloat16),
+            pltpu.SemaphoreType.DMA((pages,)),
+        ],
+        cost_estimate=cost(0, pages * PAGE_ROWS * kv_width * 16),
+        name="prepare",
+    )(user_lengths, page_slot, keys, values)
     incoming = lax.all_to_all(outgoing, slab_axes, split_axis=0, concat_axis=0, tiled=True)
     chips = lax.axis_size("x") * lax.axis_size("z")
     near, far = [
@@ -156,7 +168,8 @@
         for hop in (1, 2)
     ]
     given = jnp.stack([near, jnp.where(core == 0, own, far)])
-    partner = lax.ppermute(given, "core", [(0, 1), (1, 0)])
+    swap = [(0, 1), (1, 0)]
+    partner = lax.ppermute(given, "core", swap)
 
     slots = slab * pages + jnp.arange(pages, dtype=jnp.int32)
     page_index = jnp.arange(page_slot.shape[0], dtype=jnp.int32)
@@ -164,25 +177,34 @@
         jnp.where(page_slot[None, :] == slots[:, None], page_index[None, :] // pages, 0), axis=1
     )
 
-    attended = pl.pallas_call(
+    half_rows = jax.ShapeDtypeStruct((tokens // HALVES, queries.shape[1]), jnp.bfloat16)
+    kept, sent = pl.pallas_call(
         attend_kernel,
-        out_shape=jax.ShapeDtypeStruct(queries.shape, jnp.bfloat16),
-        in_specs=[SMEM, SMEM, VMEM, VMEM, VMEM, VMEM, VMEM],
-        out_specs=VMEM,
-        cost_estimate=cost(ATTEND_WEIGHT * 4 * queries.shape[0] * queries.shape[1] * 5 * tokens, 2 << 20),
-        compiler_params=pltpu.CompilerParams(vmem_limit_bytes=24 << 20),
+        out_shape=(half_rows, half_rows),
+        in_specs=[SMEM, VMEM, VMEM, VMEM, VMEM, VMEM],
+        out_specs=(VMEM, VMEM),
+        cost_estimate=cost(
+            ATTEND_WEIGHT * 4 * queries.shape[0] * queries.shape[1] * 5 * tokens, 2 << 20
+        ),
+        compiler_params=pltpu.CompilerParams(vmem_limit_bytes=16 << 20),
         name="attend",
-    )(place, user_lengths, queries, own, near, far, partner)
+    )(user_lengths, queries, own, near, far, partner)
+    arrived = lax.ppermute(sent, "half", swap)
+    first_half = lax.axis_index("half") == 0
+    halves = [jnp.where(first_half, kept, arrived), jnp.where(first_half, arrived, kept)]
+    quarters = lax.axis_size("quarter")
+    attended = jnp.stack([part.reshape(quarters, -1, queries.shape[1]) for part in halves], axis=1)
     attended, incoming = lax.optimization_barrier((attended, incoming))
-    attention_out = lax.all_to_all(attended, "head", split_axis=0, concat_axis=1, tiled=True)
+    exchanged = lax.all_to_all(attended, "quarter", split_axis=0, concat_axis=0, tiled=True)
+    attention_out = jnp.transpose(exchanged, (2, 1, 0, 3)).reshape(exchanged.shape[2], -1)
 
     kv_cache = pl.pallas_call(
         collect_kernel,
-        out_shape=jax.ShapeDtypeStruct((pages, 2, PAGE_ROWS, kv_width), jnp.bfloat16),
-        in_specs=[SMEM, ANY],
+        out_shape=jax.ShapeDtypeStruct((pages,) + page_block, jnp.bfloat16),
+        in_specs=[SMEM, VMEM],
         out_specs=VMEM,
-        scratch_shapes=[pltpu.SemaphoreType.DMA((pages,))],
         cost_estimate=cost(0, pages * PAGE_ROWS * kv_width * 8),
+        compiler_params=pltpu.CompilerParams(vmem_limit_bytes=4 << 20),
         name="collect",
     )(source, incoming)
     return attention_out, kv_cache
@@ -193,20 +215,13 @@
     chips = mesh.shape["slab"] // CORES
     z = next(n for n in (8, 4, 2, 1) if chips % n == 0)
     x = chips // z
-    split = Mesh(mesh.devices.reshape(x, z, CORES, y), ("x", "z", "core", "head"))
+    axes = ("x", "z", "core", "half", "quarter")
+    split = Mesh(mesh.devices.reshape(x, z, CORES, HALVES, y // HALVES), axes)
+    slab, head = axes[:3], axes[3:]
     return jax.shard_map(
         body,
         mesh=split,
-        in_specs=(
-            P(("x", "z", "core"), "head"),
-            P(("x", "z", "core"), "head"),
-            P(("x", "z", "core"), "head"),
-            P(),
-            P(),
-        ),
-        out_specs=(
-            P(("x", "z", "core", "head"), None),
-            P(("x", "z", "core"), None, None, "head"),
-        ),
+        in_specs=(P(slab, head), P(slab, head), P(slab, head), P(), P()),
+        out_specs=(P(slab + head, None), P(slab, None, None, head)),
         check_vma=False,
     )

time: 75 us -> 70.3 us (0.937)
  the two profiles are of different devices: /device:TPU:6 before, /device:TPU:56 now
where the time goes in v2:
time: 70.3 us; the launch traced here: 69.9 us
  starting transfers between devices  34.7 us (49%)
  waiting for transfers between devices  24.2 us (34%)
  Pallas kernels  6.42 us (9%)
  other arithmetic  2.03 us (3%)
  local copies, waits for them, and re-layouts  1.79 us (3%)
  between operations  0.79 us (1%)
    all_to_all x1, starting transfers between devices, body(): lax.all_to_all(outgoing, slab_axes, split_axis=0, concat_axis=0, tiled=True)  11.2 us
    ppermute x2, starting transfers between devices, body(): lax.ppermute(own, ('x', 'z'), [(i, i + hop) for i in range(chips - hop)])  10.4 us
    all_to_all x1, waiting for transfers between devices, body(): lax.all_to_all(outgoing, slab_axes, split_axis=0, concat_axis=0, tiled=True)  9.08 us
    ppermute x1, waiting for transfers between devices, body(): arrived = lax.ppermute(sent, 'half', swap)  9.06 us
    all_to_all x1, starting transfers between devices, body(): lax.all_to_all(attended, 'quarter', split_axis=0, concat_axis=0, tiled=True)  6.3 us
    ppermute x1, starting transfers between devices, body(): arrived = lax.ppermute(sent, 'half', swap)  4.71 us
    all_to_all x1, waiting for transfers between devices, body(): lax.all_to_all(attended, 'quarter', split_axis=0, concat_axis=0, tiled=True)  4.22 us
    pallas_call x1, Pallas kernels, body(): pl.pallas_call(attend_kernel, out_shape=(half_rows, half_rows), in_specs=...  3.25 us
  transfers between devices with their start and end apart: 6, of which 4 were waited for; matrix products, arithmetic and copies ran while one was open for 1% of the time, Pallas kernels for 9%

profile of v2, /device:TPU:56, one launch (start us, length us, event | category | flops | bytes accessed | tf_op | source)
XLA Modules:
  0.0 69.9 jit_solution(2806793886109767829)
XLA Ops:
  0.6 1.0 %pad_maximum_fusion.1.own_ref = bf16[2,256,256]{2,1,0:T(8,128)(2,1)S(1)} fusion(bf16[1,256,256]{2,1,0:T(8,128)(2,1)} %bitcast.13, bf16[1,256,256]{2,1,0:T(8,128)(2,1)} %bitcast.15), kind=kLoop, calls=%fused_computation.1 | loop fusion | flops 131072 | bytes 524288 | tf_op jit(solution)/shard_map/stack | solution.py:151
  1.6 6.1 %collective-permute-start.1 = (bf16[2,256,256]{2,1,0:T(8,128)(2,1)S(1)}, bf16[2,256,256]{2,1,0:T(8,128)(2,1)S(1)}, u32[]{:S(2)}, u32[]{:S(2)}) collective-permute-start(bf16[2,256,256]{2,1,0:T(8,128)(2,1)S(1)} %pad_maximum_fusion.1.own_ref), channel_id=1, source_target_pairs={{0,32},{16,48},{32,64},{48,80},{64,96},{80,112},{96,128},{112,144}... | collective-permute-start | bytes 786440 | tf_op jit(solution)/shard_map/ppermute | solution.py:167
  7.7 4.3 %collective-permute-start = (bf16[2,256,256]{2,1,0:T(8,128)(2,1)S(1)}, bf16[2,256,256]{2,1,0:T(8,128)(2,1)S(1)}, u32[]{:S(2)}, u32[]{:S(2)}) collective-permute-start(bf16[2,256,256]{2,1,0:T(8,128)(2,1)S(1)} %pad_maximum_fusion.1.own_ref), channel_id=1, source_target_pairs={{0,16},{16,32},{32,48},{48,64},{64,80},{80,96},{96,112},{112,128},... | collective-permute-start | bytes 786440 | tf_op jit(solution)/shard_map/ppermute | solution.py:167
  12.0 1.9 %prepare.1 = bf16[64,2,16,256]{3,2,1,0:T(8,128)(2,1)} custom-call(s32[4]{0:T(128)} %lengths_ref.3, s32[1024]{0:T(1024)} %slot_ref.1, bf16[256,256]{1,0:T(8,128)(2,1)} %keys_ref.1, bf16[256,256]{1,0:T(8,128)(2,1)} %values_ref.1), custom_call_target="tpu_custom_call" | custom-call | bytes 1048576 | tf_op jit(solution)/shard_map/prepare/pallas_call | solution.py:152
  13.9 0.0 copy-start.2
  14.0 0.0 copy-start.3
  14.0 11.2 %all-to-all-start = ((bf16[64,2,16,256]{3,2,1,0:T(8,128)(2,1)}), bf16[64,2,16,256]{3,2,1,0:T(8,128)(2,1)S(1)}, u32[]{:S(2)}, u32[]{:S(2)}) async-start(bf16[64,2,16,256]{3,2,1,0:T(8,128)(2,1)} %prepare.1), calls=%async_computation | async-start | bytes 2097152 | tf_op jit(solution)/shard_map/all_to_all | solution.py:164
  25.2 0.0 collective-permute-done.1.far_ref
  25.2 0.0 copy-done.2
  25.2 0.0 copy-done.3
  25.2 0.0 collective-permute-done.near_ref
  25.3 0.0 copy-start
  25.3 0.0 copy-start.1
  25.3 0.1 pad_maximum_fusion
  25.3 2.1 %collective-permute-start.2 = (bf16[2,2,256,256]{3,2,1,0:T(8,128)(2,1)S(1)}, bf16[2,2,256,256]{3,2,1,0:T(8,128)(2,1)S(1)}, u32[]{:S(2)}, u32[]{:S(2)}) collective-permute-start(bf16[2,2,256,256]{3,2,1,0:T(8,128)(2,1)S(1)} %pad_maximum_fusion), channel_id=1, source_target_pairs={{0,8},{8,0},{1,9},{9,1},{2,10},{10,2},{3,11},{11,3},{4,12},{12,4},... | collective-permute-start | bytes 1572872 | tf_op jit(solution)/shard_map/ppermute | solution.py:172
  27.4 1.8 %collective-permute-done.2.partner_ref = bf16[2,2,256,256]{3,2,1,0:T(8,128)(2,1)S(1)} collective-permute-done((bf16[2,2,256,256]{3,2,1,0:T(8,128)(2,1)S(1)}, bf16[2,2,256,256]{3,2,1,0:T(8,128)(2,1)S(1)}, u32[]{:S(2)}, u32[]{:S(2)}) %collective-permute-start.2) | collective-permute-done | bytes 524320 | tf_op jit(solution)/shard_map/ppermute | solution.py:172
  29.3 0.0 copy-done
  29.3 0.0 copy-done.1
  29.3 3.2 %attend.1 = (bf16[128,512]{1,0:T(8,128)(2,1)S(1)}, bf16[128,512]{1,0:T(8,128)(2,1)S(1)}) custom-call(s32[4]{0:T(128)S(1)} %copy-done, bf16[256,512]{1,0:T(8,128)(2,1)S(1)} %copy-done.1, bf16[2,256,256]{2,1,0:T(8,128)(2,1)S(1)} %pad_maximum_fusion.1.own_ref, bf16[2,256,256]{2,1,0:T(8,128)(2,1)S(1)} %collective-permute-done.near_ref, ...), custom_call_target="tpu_custom_call" | custom-call | flops 9395240960 | bytes 2097152 | tf_op jit(solution)/shard_map/attend/pallas_call | solution.py:181
  32.5 4.7 %collective-permute-start.3 = (bf16[128,512]{1,0:T(8,128)(2,1)S(1)}, bf16[128,512]{1,0:T(8,128)(2,1)S(1)}, u32[]{:S(2)}, u32[]{:S(2)}) collective-permute-start(bf16[128,512]{1,0:T(8,128)(2,1)S(1)} %get-tuple-element.7), channel_id=1, source_target_pairs={{0,4},{4,0},{1,5},{5,1},{2,6},{6,2},{3,7},{7,3},{8,12},{12,8},{9,1... | collective-permute-start | bytes 393224 | tf_op jit(solution)/shard_map/ppermute | solution.py:192
  37.3 9.1 %collective-permute-done.3 = bf16[128,512]{1,0:T(8,128)(2,1)S(1)} collective-permute-done((bf16[128,512]{1,0:T(8,128)(2,1)S(1)}, bf16[128,512]{1,0:T(8,128)(2,1)S(1)}, u32[]{:S(2)}, u32[]{:S(2)}) %collective-permute-start.3) | collective-permute-done | bytes 131104 | tf_op jit(solution)/shard_map/ppermute | solution.py:192
  46.3 0.7 %pad_maximum_fusion.2 = bf16[4,2,32,512]{3,2,1,0:T(8,128)(2,1)} fusion(bf16[4,1,32,512]{3,2,1,0:T(8,128)(2,1)S(1)} %bitcast.19, bf16[4,1,32,512]{3,2,1,0:T(8,128)(2,1)S(1)} %bitcast.18), kind=kLoop, calls=%fused_computation.2 | loop fusion | flops 131072 | bytes 524288 | tf_op jit(solution)/shard_map/stack | solution.py:196
  47.1 9.1 %all-to-all-done.in_ref = bf16[64,2,16,256]{3,2,1,0:T(8,128)(2,1)S(1)} async-done(((bf16[64,2,16,256]{3,2,1,0:T(8,128)(2,1)}), bf16[64,2,16,256]{3,2,1,0:T(8,128)(2,1)S(1)}, u32[]{:S(2)}, u32[]{:S(2)}) %all-to-all-start) | async-done | bytes 1048608 | tf_op jit(solution)/shard_map/all_to_all | solution.py:164
  56.2 6.3 %all-to-all-start.1 = ((bf16[4,2,32,512]{3,2,1,0:T(8,128)(2,1)}), bf16[4,2,32,512]{3,2,1,0:T(8,128)(2,1)S(1)}, u32[]{:S(2)}, u32[]{:S(2)}) async-start(bf16[4,2,32,512]{3,2,1,0:T(8,128)(2,1)} %pad_maximum_fusion.2), calls=%async_computation.1 | async-start | bytes 524288 | tf_op jit(solution)/shard_map/all_to_all | solution.py:198
  62.5 0.0 copy-start.4
  62.5 0.7 copy-done.4
  63.1 0.2 select_reduce_fusion.source_ref
  63.3 1.3 %collect.1 = bf16[16,2,16,256]{3,2,1,0:T(8,128)(2,1)} custom-call(s32[16]{0:T(128)S(1)} %select_reduce_fusion.source_ref, bf16[64,2,16,256]{3,2,1,0:T(8,128)(2,1)S(1)} %all-to-all-done.in_ref), custom_call_target="tpu_custom_call" | custom-call | bytes 524288 | tf_op jit(solution)/shard_map/collect/pallas_call | solution.py:201
  64.6 4.2 %all-to-all-done.1 = bf16[4,2,32,512]{3,2,1,0:T(8,128)(2,1)S(1)} async-done(((bf16[4,2,32,512]{3,2,1,0:T(8,128)(2,1)}), bf16[4,2,32,512]{3,2,1,0:T(8,128)(2,1)S(1)}, u32[]{:S(2)}, u32[]{:S(2)}) %all-to-all-start.1) | async-done | bytes 262176 | tf_op jit(solution)/shard_map/all_to_all | solution.py:198
  68.8 0.2 copy.15
  69.0 0.9 %reshape.49 = bf16[32,4096]{1,0:T(8,128)(2,1)} reshape(bf16[32,2,4,512]{3,2,1,0:T(4,128)(2,1)S(1)} %copy.15) | data formatting | bytes 524288 | tf_op jit(solution)/shard_map/reshape | solution.py:199
  (4 shorter events, 0.1 us)
Async XLA Ops:
  1.6 23.5 %collective-permute-start.1 = (bf16[2,256,256]{2,1,0:T(8,128)(2,1)S(1)}, bf16[2,256,256]{2,1,0:T(8,128)(2,1)S(1)}, u32[]{:S(2)}, u32[]{:S(2)}) collective-permute-start(bf16[2,256,256]{2,1,0:T(8,128)(2,1)S(1)} %pad_maximum_fusion.1.own_ref), channel_id=1, source_target_pairs={{0,32},{16,48},{32,64},{48,80},{64,96},{80,112},{96,128},{112,144}... | collective-permute-start | bytes 786440 | tf_op jit(solution)/shard_map/ppermute | solution.py:167
  7.7 17.5 %collective-permute-start = (bf16[2,256,256]{2,1,0:T(8,128)(2,1)S(1)}, bf16[2,256,256]{2,1,0:T(8,128)(2,1)S(1)}, u32[]{:S(2)}, u32[]{:S(2)}) collective-permute-start(bf16[2,256,256]{2,1,0:T(8,128)(2,1)S(1)} %pad_maximum_fusion.1.own_ref), channel_id=1, source_target_pairs={{0,16},{16,32},{32,48},{48,64},{64,80},{80,96},{96,112},{112,128},... | collective-permute-start | bytes 786440 | tf_op jit(solution)/shard_map/ppermute | solution.py:167
  13.9 11.2 %copy-start.2 = (bf16[256,256]{1,0:T(8,128)(2,1)S(1)}, bf16[256,256]{1,0:T(8,128)(2,1)}, u32[]{:S(2)}) copy-start(bf16[256,256]{1,0:T(8,128)(2,1)} %values_ref.1) | copy-start | bytes 393220
  14.0 11.2 %copy-start.3 = (bf16[256,256]{1,0:T(8,128)(2,1)S(1)}, bf16[256,256]{1,0:T(8,128)(2,1)}, u32[]{:S(2)}) copy-start(bf16[256,256]{1,0:T(8,128)(2,1)} %keys_ref.1) | copy-start | bytes 393220
  14.0 42.2 %all-to-all-start = ((bf16[64,2,16,256]{3,2,1,0:T(8,128)(2,1)}), bf16[64,2,16,256]{3,2,1,0:T(8,128)(2,1)S(1)}, u32[]{:S(2)}, u32[]{:S(2)}) async-start(bf16[64,2,16,256]{3,2,1,0:T(8,128)(2,1)} %prepare.1), calls=%async_computation | async-start | bytes 2097152 | tf_op jit(solution)/shard_map/all_to_all | solution.py:164
  25.3 4.0 %copy-start = (s32[4]{0:T(128)S(1)}, s32[4]{0:T(128)}, u32[]{:S(2)}) copy-start(s32[4]{0:T(128)} %lengths_ref.3) | copy-start | bytes 52
  25.3 4.0 %copy-start.1 = (bf16[256,512]{1,0:T(8,128)(2,1)S(1)}, bf16[256,512]{1,0:T(8,128)(2,1)}, u32[]{:S(2)}) copy-start(bf16[256,512]{1,0:T(8,128)(2,1)} %queries_ref.1) | copy-start | bytes 786436
  25.3 3.9 %collective-permute-start.2 = (bf16[2,2,256,256]{3,2,1,0:T(8,128)(2,1)S(1)}, bf16[2,2,256,256]{3,2,1,0:T(8,128)(2,1)S(1)}, u32[]{:S(2)}, u32[]{:S(2)}) collective-permute-start(bf16[2,2,256,256]{3,2,1,0:T(8,128)(2,1)S(1)} %pad_maximum_fusion), channel_id=1, source_target_pairs={{0,8},{8,0},{1,9},{9,1},{2,10},{10,2},{3,11},{11,3},{4,12},{12,4},... | collective-permute-start | bytes 1572872 | tf_op jit(solution)/shard_map/ppermute | solution.py:172
  32.5 13.8 %collective-permute-start.3 = (bf16[128,512]{1,0:T(8,128)(2,1)S(1)}, bf16[128,512]{1,0:T(8,128)(2,1)S(1)}, u32[]{:S(2)}, u32[]{:S(2)}) collective-permute-start(bf16[128,512]{1,0:T(8,128)(2,1)S(1)} %get-tuple-element.7), channel_id=1, source_target_pairs={{0,4},{4,0},{1,5},{5,1},{2,6},{6,2},{3,7},{7,3},{8,12},{12,8},{9,1... | collective-permute-start | bytes 393224 | tf_op jit(solution)/shard_map/ppermute | solution.py:192
  56.2 12.7 %all-to-all-start.1 = ((bf16[4,2,32,512]{3,2,1,0:T(8,128)(2,1)}), bf16[4,2,32,512]{3,2,1,0:T(8,128)(2,1)S(1)}, u32[]{:S(2)}, u32[]{:S(2)}) async-start(bf16[4,2,32,512]{3,2,1,0:T(8,128)(2,1)} %pad_maximum_fusion.2), calls=%async_computation.1 | async-start | bytes 524288 | tf_op jit(solution)/shard_map/all_to_all | solution.py:198
  62.5 0.7 copy-start.4

commit v3 on v2

--- a/solution.py
+++ b/solution.py
@@ -16,7 +16,7 @@
 MASKED = -1e30
 CORES = 2
 HALVES = 2
-ATTEND_WEIGHT = 14
+ATTEND_WEIGHT = 17
 
 VMEM = pl.BlockSpec(memory_space=pltpu.VMEM)
 SMEM = pl.BlockSpec(memory_space=pltpu.SMEM)
@@ -76,14 +76,17 @@
 
 
 def attend_kernel(
-    lengths_ref, queries_ref, own_ref, near_ref, far_ref, partner_ref, kept_ref, sent_ref
+    mine, lengths_ref, queries_ref, own_ref, near_ref, far_ref, partner_ref, out_ref, parts_ref
 ):
     slab, core = here()
     tokens = queries_ref.shape[0]
     kv_local = own_ref.shape[2] // HEAD_DIM
     group = queries_ref.shape[1] // (kv_local * HEAD_DIM)
     first_core = core == 0
-    first_half = lax.axis_index("half") == 0
+    half, quarter = lax.axis_index("half"), lax.axis_index("quarter")
+    quarters, part_rows = out_ref.shape[:2]
+    rows = quarters * part_rows
+    row_start = pl.multiple_of((half if mine else 1 - half) * rows, rows)
     pieces = [
         (own_ref, 0),
         (near_ref, 2),
@@ -91,15 +94,15 @@
         (partner_ref.at[0], jnp.where(first_core, 1, 3)),
         (partner_ref.at[1], jnp.where(first_core, 3, 1)),
     ]
-    row = lax.broadcasted_iota(jnp.int32, (tokens, 1), 0)
-    column = lax.broadcasted_iota(jnp.int32, (tokens, tokens), 1)
+    row = row_start + lax.broadcasted_iota(jnp.int32, (rows, 1), 0)
+    column = lax.broadcasted_iota(jnp.int32, (rows, tokens), 1)
     first = user_first(slab * tokens + row, lengths_ref)
-    causal = column <= lax.broadcasted_iota(jnp.int32, (tokens, tokens), 0)
+    causal = column <= row
     for g in range(kv_local):
         kv_columns = slice(g * HEAD_DIM, (g + 1) * HEAD_DIM)
         for r in range(group):
             h = g * group + r
-            query = queries_ref[:, h * HEAD_DIM : (h + 1) * HEAD_DIM]
+            query = queries_ref[pl.ds(row_start, rows), h * HEAD_DIM : (h + 1) * HEAD_DIM]
             scores = []
             for ref, back in pieces:
                 s = lax.dot_general(
@@ -128,11 +131,31 @@
                 total = shifted if total is None else total + shifted
                 mixed = part if mixed is None else mixed + part
             denominators = jnp.sum(total, axis=1, keepdims=True)
-            result = (mixed / denominators).astype(kept_ref.dtype)
-            lower, upper = result[: tokens // HALVES], result[tokens // HALVES :]
+            result = (mixed / denominators).astype(out_ref.dtype)
             columns = slice(h * HEAD_DIM, (h + 1) * HEAD_DIM)
-            kept_ref[:, columns] = jnp.where(first_half, lower, upper)
-            sent_ref[:, columns] = jnp.where(first_half, upper, lower)
+            for target in range(quarters):
+                parts_ref[target, :, columns] = result[
+                    target * part_rows : (target + 1) * part_rows
+                ]
+    for e in range(quarters):
+        out_ref[e] = parts_ref[quarter ^ e]
+
+
+def pair_kernel(kept_ref, arrived_ref, *out_refs):
+    half = lax.axis_index("half")
+    for e, ref in enumerate(out_refs):
+        ref[half] = kept_ref[e]
+        ref[1 - half] = arrived_ref[e]
+
+
+def join_kernel(*refs):
+    *in_refs, out_ref = refs
+    quarter = lax.axis_index("quarter")
+    width = in_refs[0].shape[2]
+    for e, ref in enumerate(in_refs):
+        for half in range(HALVES):
+            start = (half * len(in_refs) + (quarter ^ e)) * width
+            out_ref[:, pl.ds(pl.multiple_of(start, width), width)] = ref[half]
 
 
 def cost(flops, moved):
@@ -161,12 +184,12 @@
         cost_estimate=cost(0, pages * PAGE_ROWS * kv_width * 16),
         name="prepare",
     )(user_lengths, page_slot, keys, values)
+    chips = lax.axis_size("x") * lax.axis_size("z")
+    forward = [(i, i + 1) for i in range(chips - 1)]
+    near = lax.ppermute(own, ("x", "z"), forward)
+    near, outgoing = lax.optimization_barrier((near, outgoing))
+    far = lax.ppermute(near, ("x", "z"), forward)
     incoming = lax.all_to_all(outgoing, slab_axes, split_axis=0, concat_axis=0, tiled=True)
-    chips = lax.axis_size("x") * lax.axis_size("z")
-    near, far = [
-        lax.ppermute(own, ("x", "z"), [(i, i + hop) for i in range(chips - hop)])
-        for hop in (1, 2)
-    ]
     given = jnp.stack([near, jnp.where(core == 0, own, far)])
     swap = [(0, 1), (1, 0)]
     partner = lax.ppermute(given, "core", swap)
@@ -177,27 +200,39 @@
         jnp.where(page_slot[None, :] == slots[:, None], page_index[None, :] // pages, 0), axis=1
     )
 
-    half_rows = jax.ShapeDtypeStruct((tokens // HALVES, queries.shape[1]), jnp.bfloat16)
-    kept, sent = pl.pallas_call(
-        attend_kernel,
-        out_shape=(half_rows, half_rows),
-        in_specs=[SMEM, VMEM, VMEM, VMEM, VMEM, VMEM],
-        out_specs=(VMEM, VMEM),
-        cost_estimate=cost(
-            ATTEND_WEIGHT * 4 * queries.shape[0] * queries.shape[1] * 5 * tokens, 2 << 20
-        ),
-        compiler_params=pltpu.CompilerParams(vmem_limit_bytes=16 << 20),
-        name="attend",
-    )(user_lengths, queries, own, near, far, partner)
+    quarters = lax.axis_size("quarter")
+    part_rows = tokens // (HALVES * quarters)
+    parts = jax.ShapeDtypeStruct((quarters, part_rows, queries.shape[1]), jnp.bfloat16)
+    pair = jax.ShapeDtypeStruct((HALVES,) + parts.shape[1:], jnp.bfloat16)
+    sent, kept = [
+        pl.pallas_call(
+            functools.partial(attend_kernel, mine),
+            out_shape=parts,
+            in_specs=[SMEM, VMEM, VMEM, VMEM, VMEM, VMEM],
+            out_specs=VMEM,
+            scratch_shapes=[pltpu.VMEM(parts.shape, jnp.bfloat16)],
+            cost_estimate=cost(
+                ATTEND_WEIGHT * 2 * queries.shape[0] * queries.shape[1] * 5 * tokens, 2 << 20
+            ),
+            compiler_params=pltpu.CompilerParams(vmem_limit_bytes=16 << 20),
+            name="attend_kept" if mine else "attend_sent",
+        )(user_lengths, queries, own, near, far, partner)
+        for mine in (False, True)
+    ]
     arrived = lax.ppermute(sent, "half", swap)
-    first_half = lax.axis_index("half") == 0
-    halves = [jnp.where(first_half, kept, arrived), jnp.where(first_half, arrived, kept)]
-    quarters = lax.axis_size("quarter")
-    attended = jnp.stack([part.reshape(quarters, -1, queries.shape[1]) for part in halves], axis=1)
-    attended, incoming = lax.optimization_barrier((attended, incoming))
-    exchanged = lax.all_to_all(attended, "quarter", split_axis=0, concat_axis=0, tiled=True)
-    attention_out = jnp.transpose(exchanged, (2, 1, 0, 3)).reshape(exchanged.shape[2], -1)
-
+    pairs = pl.pallas_call(
+        pair_kernel,
+        out_shape=(pair,) * quarters,
+        in_specs=[VMEM, VMEM],
+        out_specs=(VMEM,) * quarters,
+        cost_estimate=cost(0, tokens * queries.shape[1] * 4),
+        compiler_params=pltpu.CompilerParams(vmem_limit_bytes=4 << 20),
+        name="pair",
+    )(kept, arrived)
+    gathered = [pairs[0]] + [
+        lax.ppermute(pairs[e], "quarter", [(i, i ^ e) for i in range(quarters)])
+        for e in range(1, quarters)
+    ]
     kv_cache = pl.pallas_call(
         collect_kernel,
         out_shape=jax.ShapeDtypeStruct((pages,) + page_block, jnp.bfloat16),
@@ -207,6 +242,19 @@
         compiler_params=pltpu.CompilerParams(vmem_limit_bytes=4 << 20),
         name="collect",
     )(source, incoming)
+    gathered[-1], kv_cache = lax.optimization_barrier((gathered[-1], kv_cache))
+    attention_out = pl.pallas_call(
+        join_kernel,
+        out_shape=jax.ShapeDtypeStruct(
+            (part_rows, HALVES * quarters * queries.shape[1]), jnp.bfloat16
+        ),
+        in_specs=[VMEM] * quarters,
+        out_specs=VMEM,
+        cost_estimate=cost(0, tokens * queries.shape[1] * 4),
+        compiler_params=pltpu.CompilerParams(vmem_limit_bytes=4 << 20),
+        name="join",
+    )(*gathered)
+
     return attention_out, kv_cache
 
 

time: 70.3 us -> 67.9 us (0.966)
  the two profiles are of different devices: /device:TPU:56 before, /device:TPU:6 now
where the time goes in v3:
time: 67.9 us; the launch traced here: 67.5 us
  starting transfers between devices  37.2 us (55%)
  waiting for transfers between devices  19.5 us (29%)
  Pallas kernels  8.65 us (13%)
  other arithmetic  1.28 us (2%)
  between operations  0.82 us (1%)
    ppermute x3, starting transfers between devices, body(): lax.ppermute(pairs[e], 'quarter', [(i, i ^ e) for i in range(quarters)])  12.4 us
    ppermute x1, waiting for transfers between devices, body(): near = lax.ppermute(own, ('x', 'z'), forward)  11.3 us
    all_to_all x1, starting transfers between devices, body(): lax.all_to_all(outgoing, slab_axes, split_axis=0, concat_axis=0, tiled=True)  8.98 us
    ppermute x1, starting transfers between devices, body(): arrived = lax.ppermute(sent, 'half', swap)  7.73 us
    pallas_call x2, Pallas kernels, body(): pl.pallas_call(functools.partial(attend_kernel, mine), out_shape=parts, i...  4.72 us
    ppermute x3, waiting for transfers between devices, body(): lax.ppermute(pairs[e], 'quarter', [(i, i ^ e) for i in range(quarters)])  4.31 us
    ppermute x1, starting transfers between devices, body(): near = lax.ppermute(own, ('x', 'z'), forward)  4.28 us
    ppermute x1, starting transfers between devices, body(): partner = lax.ppermute(given, 'core', swap)  1.92 us
  transfers between devices with their start and end apart: 8, of which 5 were waited for; matrix products, arithmetic and copies ran while one was open for 0% of the time, Pallas kernels for 12%

profile of v3, /device:TPU:6, one launch (start us, length us, event | category | flops | bytes accessed | tf_op | source)
XLA Modules:
  0.0 67.5 jit_solution(7314845836975646334)
XLA Ops:
  0.6 1.0 %pad_maximum_fusion.1.own_ref = bf16[2,256,256]{2,1,0:T(8,128)(2,1)S(1)} fusion(bf16[1,256,256]{2,1,0:T(8,128)(2,1)} %bitcast.6, bf16[1,256,256]{2,1,0:T(8,128)(2,1)} %bitcast.8), kind=kLoop, calls=%fused_computation.1 | loop fusion | flops 131072 | bytes 524288 | tf_op jit(solution)/shard_map/stack | solution.py:174
  1.6 4.3 %collective-permute-start = (bf16[2,256,256]{2,1,0:T(8,128)(2,1)S(1)}, bf16[2,256,256]{2,1,0:T(8,128)(2,1)S(1)}, u32[]{:S(2)}, u32[]{:S(2)}) collective-permute-start(bf16[2,256,256]{2,1,0:T(8,128)(2,1)S(1)} %pad_maximum_fusion.1.own_ref), channel_id=1, source_target_pairs={{0,16},{16,32},{32,48},{48,64},{64,80},{80,96},{96,112},{112,128},... | collective-permute-start | bytes 786440 | tf_op jit(solution)/shard_map/ppermute | solution.py:189
  5.9 1.9 %prepare.1 = bf16[64,2,16,256]{3,2,1,0:T(8,128)(2,1)} custom-call(s32[4]{0:T(128)} %lengths_ref.5, s32[1024]{0:T(1024)} %slot_ref.1, bf16[256,256]{1,0:T(8,128)(2,1)} %keys_ref.1, bf16[256,256]{1,0:T(8,128)(2,1)} %values_ref.1), custom_call_target="tpu_custom_call" | custom-call | bytes 1048576 | tf_op jit(solution)/shard_map/prepare/pallas_call | solution.py:175
  7.8 11.3 %collective-permute-done.near_ref = bf16[2,256,256]{2,1,0:T(8,128)(2,1)S(1)} collective-permute-done((bf16[2,256,256]{2,1,0:T(8,128)(2,1)S(1)}, bf16[2,256,256]{2,1,0:T(8,128)(2,1)S(1)}, u32[]{:S(2)}, u32[]{:S(2)}) %collective-permute-start) | collective-permute-done | bytes 262176 | tf_op jit(solution)/shard_map/ppermute | solution.py:189
  19.1 1.9 %collective-permute-start.1 = (bf16[2,256,256]{2,1,0:T(8,128)(2,1)S(1)}, bf16[2,256,256]{2,1,0:T(8,128)(2,1)S(1)}, u32[]{:S(2)}, u32[]{:S(2)}) collective-permute-start(bf16[2,256,256]{2,1,0:T(8,128)(2,1)S(1)} %collective-permute-done.near_ref), channel_id=1, source_target_pairs={{0,16},{16,32},{32,48},{48,64},{64,80},{80,96},{96,112},{112,128},... | collective-permute-start | bytes 786440 | tf_op jit(solution)/shard_map/ppermute | solution.py:191
  21.1 0.0 copy-start.2
  21.1 0.0 copy-start.3
  21.1 9.0 %all-to-all-start = ((bf16[64,2,16,256]{3,2,1,0:T(8,128)(2,1)}), bf16[64,2,16,256]{3,2,1,0:T(8,128)(2,1)S(1)}, u32[]{:S(2)}, u32[]{:S(2)}) async-start(bf16[64,2,16,256]{3,2,1,0:T(8,128)(2,1)} %prepare.1), calls=%async_computation | async-start | bytes 2097152 | tf_op jit(solution)/shard_map/all_to_all | solution.py:192
  30.1 0.5 collective-permute-done.1.far_ref
  30.6 0.0 copy-done.2
  30.6 0.0 copy-done.3
  30.7 0.0 copy-start.1
  30.7 0.1 pad_maximum_fusion
  30.7 1.9 %collective-permute-start.2 = (bf16[2,2,256,256]{3,2,1,0:T(8,128)(2,1)S(1)}, bf16[2,2,256,256]{3,2,1,0:T(8,128)(2,1)S(1)}, u32[]{:S(2)}, u32[]{:S(2)}) collective-permute-start(bf16[2,2,256,256]{3,2,1,0:T(8,128)(2,1)S(1)} %pad_maximum_fusion), channel_id=1, source_target_pairs={{0,8},{8,0},{1,9},{9,1},{2,10},{10,2},{3,11},{11,3},{4,12},{12,4},... | collective-permute-start | bytes 1572872 | tf_op jit(solution)/shard_map/ppermute | solution.py:195
  32.7 0.0 copy-start
  32.7 1.8 %collective-permute-done.2.partner_ref = bf16[2,2,256,256]{3,2,1,0:T(8,128)(2,1)S(1)} collective-permute-done((bf16[2,2,256,256]{3,2,1,0:T(8,128)(2,1)S(1)}, bf16[2,2,256,256]{3,2,1,0:T(8,128)(2,1)S(1)}, u32[]{:S(2)}, u32[]{:S(2)}) %collective-permute-start.2) | collective-permute-done | bytes 524320 | tf_op jit(solution)/shard_map/ppermute | solution.py:195
  34.5 0.0 copy-done.1
  34.5 0.0 copy-done
  34.5 2.4 %attend_sent.1 = bf16[4,32,512]{2,1,0:T(8,128)(2,1)S(1)} custom-call(s32[4]{0:T(128)S(1)} %copy-done, bf16[256,512]{1,0:T(8,128)(2,1)S(1)} %copy-done.1, bf16[2,256,256]{2,1,0:T(8,128)(2,1)S(1)} %pad_maximum_fusion.1.own_ref, bf16[2,256,256]{2,1,0:T(8,128)(2,1)S(1)} %collective-permute-done.near_ref, ...), custom_call_target="tpu_custom_call" | custom-call | flops 5704253440 | bytes 2097152 | tf_op jit(solution)/shard_map/attend_sent/pallas_call | solution.py:208
  36.9 7.7 %collective-permute-start.3 = (bf16[4,32,512]{2,1,0:T(8,128)(2,1)S(1)}, bf16[4,32,512]{2,1,0:T(8,128)(2,1)S(1)}, u32[]{:S(2)}, u32[]{:S(2)}) collective-permute-start(bf16[4,32,512]{2,1,0:T(8,128)(2,1)S(1)} %attend_sent.1), channel_id=1, source_target_pairs={{0,4},{4,0},{1,5},{5,1},{2,6},{6,2},{3,7},{7,3},{8,12},{12,8},{9,1... | collective-permute-start | bytes 393224 | tf_op jit(solution)/shard_map/ppermute | solution.py:222
  44.7 2.4 %attend_kept.1.kept_ref = bf16[4,32,512]{2,1,0:T(8,128)(2,1)S(1)} custom-call(s32[4]{0:T(128)S(1)} %copy-done, bf16[256,512]{1,0:T(8,128)(2,1)S(1)} %copy-done.1, bf16[2,256,256]{2,1,0:T(8,128)(2,1)S(1)} %pad_maximum_fusion.1.own_ref, bf16[2,256,256]{2,1,0:T(8,128)(2,1)S(1)} %collective-permute-done.near_ref, ...), custom_call_target="tpu_custom_call" | custom-call | flops 5704253440 | bytes 2097152 | tf_op jit(solution)/shard_map/attend_kept/pallas_call | solution.py:208
  47.0 1.5 %collective-permute-done.3.arrived_ref = bf16[4,32,512]{2,1,0:T(8,128)(2,1)S(1)} collective-permute-done((bf16[4,32,512]{2,1,0:T(8,128)(2,1)S(1)}, bf16[4,32,512]{2,1,0:T(8,128)(2,1)S(1)}, u32[]{:S(2)}, u32[]{:S(2)}) %collective-permute-start.3) | collective-permute-done | bytes 131104 | tf_op jit(solution)/shard_map/ppermute | solution.py:222
  48.6 0.0 copy-start.4
  48.6 5.9 %collective-permute-start.4 = (bf16[2,32,512]{2,1,0:T(8,128)(2,1)S(1)}, bf16[2,32,512]{2,1,0:T(8,128)(2,1)S(1)}, u32[]{:S(2)}, u32[]{:S(2)}) collective-permute-start(bf16[2,32,512]{2,1,0:T(8,128)(2,1)S(1)} %get-tuple-element.12), channel_id=1, source_target_pairs={{0,1},{1,0},{2,3},{3,2},{4,5},{5,4},{6,7},{7,6},{8,9},{9,8},{10,11... | collective-permute-start | bytes 196616 | tf_op jit(solution)/shard_map/ppermute | solution.py:233
  54.5 4.3 %collective-permute-start.5 = (bf16[2,32,512]{2,1,0:T(8,128)(2,1)S(1)}, bf16[2,32,512]{2,1,0:T(8,128)(2,1)S(1)}, u32[]{:S(2)}, u32[]{:S(2)}) collective-permute-start(bf16[2,32,512]{2,1,0:T(8,128)(2,1)S(1)} %get-tuple-element.13), channel_id=1, source_target_pairs={{0,2},{1,3},{2,0},{3,1},{4,6},{5,7},{6,4},{7,5},{8,10},{9,11},{10,... | collective-permute-start | bytes 196616 | tf_op jit(solution)/shard_map/ppermute | solution.py:233
  58.8 2.2 %collective-permute-start.6 = (bf16[2,32,512]{2,1,0:T(8,128)(2,1)S(1)}, bf16[2,32,512]{2,1,0:T(8,128)(2,1)S(1)}, u32[]{:S(2)}, u32[]{:S(2)}) collective-permute-start(bf16[2,32,512]{2,1,0:T(8,128)(2,1)S(1)} %get-tuple-element.14), channel_id=1, source_target_pairs={{0,3},{1,2},{2,1},{3,0},{4,7},{5,6},{6,5},{7,4},{8,11},{9,10},{10,... | collective-permute-start | bytes 196616 | tf_op jit(solution)/shard_map/ppermute | solution.py:233
  61.0 0.0 copy-done.4
  61.0 0.2 select_reduce_fusion.source_ref
  61.2 0.0 all-to-all-done.in_ref
  61.2 1.3 %collect.1 = bf16[16,2,16,256]{3,2,1,0:T(8,128)(2,1)} custom-call(s32[16]{0:T(128)S(1)} %select_reduce_fusion.source_ref, bf16[64,2,16,256]{3,2,1,0:T(8,128)(2,1)S(1)} %all-to-all-done.in_ref), custom_call_target="tpu_custom_call" | custom-call | bytes 524288 | tf_op jit(solution)/shard_map/collect/pallas_call | solution.py:236
  62.4 4.3 %collective-permute-done.6.refs_3_ = bf16[2,32,512]{2,1,0:T(8,128)(2,1)S(1)} collective-permute-done((bf16[2,32,512]{2,1,0:T(8,128)(2,1)S(1)}, bf16[2,32,512]{2,1,0:T(8,128)(2,1)S(1)}, u32[]{:S(2)}, u32[]{:S(2)}) %collective-permute-start.6) | collective-permute-done | bytes 65568 | tf_op jit(solution)/shard_map/ppermute | solution.py:233
  66.8 0.0 collective-permute-done.4.refs_1_
  66.8 0.0 collective-permute-done.5.refs_2_
  66.8 0.7 %join.1 = bf16[32,4096]{1,0:T(8,128)(2,1)} custom-call(bf16[2,32,512]{2,1,0:T(8,128)(2,1)S(1)} %get-tuple-element.11.refs_0_, bf16[2,32,512]{2,1,0:T(8,128)(2,1)S(1)} %collective-permute-done.4.refs_1_, bf16[2,32,512]{2,1,0:T(8,128)(2,1)S(1)} %collective-permute-done.5.refs_2_, bf16[2,32,512]{2,1,0:T(8,128)(2,1)S(1)} %collective-permute-done.6.refs_3_), custom_call_target="tpu_custom_call" | custom-call | bytes 524288 | tf_op jit(solution)/shard_map/join/pallas_call | solution.py:246
  (4 shorter events, 0.1 us)
Async XLA Ops:
  1.6 17.5 %collective-permute-start = (bf16[2,256,256]{2,1,0:T(8,128)(2,1)S(1)}, bf16[2,256,256]{2,1,0:T(8,128)(2,1)S(1)}, u32[]{:S(2)}, u32[]{:S(2)}) collective-permute-start(bf16[2,256,256]{2,1,0:T(8,128)(2,1)S(1)} %pad_maximum_fusion.1.own_ref), channel_id=1, source_target_pairs={{0,16},{16,32},{32,48},{48,64},{64,80},{80,96},{96,112},{112,128},... | collective-permute-start | bytes 786440 | tf_op jit(solution)/shard_map/ppermute | solution.py:189
  19.1 11.5 %collective-permute-start.1 = (bf16[2,256,256]{2,1,0:T(8,128)(2,1)S(1)}, bf16[2,256,256]{2,1,0:T(8,128)(2,1)S(1)}, u32[]{:S(2)}, u32[]{:S(2)}) collective-permute-start(bf16[2,256,256]{2,1,0:T(8,128)(2,1)S(1)} %collective-permute-done.near_ref), channel_id=1, source_target_pairs={{0,16},{16,32},{32,48},{48,64},{64,80},{80,96},{96,112},{112,128},... | collective-permute-start | bytes 786440 | tf_op jit(solution)/shard_map/ppermute | solution.py:191
  21.1 9.6 %copy-start.2 = (bf16[256,256]{1,0:T(8,128)(2,1)S(1)}, bf16[256,256]{1,0:T(8,128)(2,1)}, u32[]{:S(2)}) copy-start(bf16[256,256]{1,0:T(8,128)(2,1)} %values_ref.1) | copy-start | bytes 393220
  21.1 9.6 %copy-start.3 = (bf16[256,256]{1,0:T(8,128)(2,1)S(1)}, bf16[256,256]{1,0:T(8,128)(2,1)}, u32[]{:S(2)}) copy-start(bf16[256,256]{1,0:T(8,128)(2,1)} %keys_ref.1) | copy-start | bytes 393220
  21.1 40.1 %all-to-all-start = ((bf16[64,2,16,256]{3,2,1,0:T(8,128)(2,1)}), bf16[64,2,16,256]{3,2,1,0:T(8,128)(2,1)S(1)}, u32[]{:S(2)}, u32[]{:S(2)}) async-start(bf16[64,2,16,256]{3,2,1,0:T(8,128)(2,1)} %prepare.1), calls=%async_computation | async-start | bytes 2097152 | tf_op jit(solution)/shard_map/all_to_all | solution.py:192
  30.7 3.9 %copy-start.1 = (bf16[256,512]{1,0:T(8,128)(2,1)S(1)}, bf16[256,512]{1,0:T(8,128)(2,1)}, u32[]{:S(2)}) copy-start(bf16[256,512]{1,0:T(8,128)(2,1)} %queries_ref.3) | copy-start | bytes 786436
  30.7 3.8 %collective-permute-start.2 = (bf16[2,2,256,256]{3,2,1,0:T(8,128)(2,1)S(1)}, bf16[2,2,256,256]{3,2,1,0:T(8,128)(2,1)S(1)}, u32[]{:S(2)}, u32[]{:S(2)}) collective-permute-start(bf16[2,2,256,256]{3,2,1,0:T(8,128)(2,1)S(1)} %pad_maximum_fusion), channel_id=1, source_target_pairs={{0,8},{8,0},{1,9},{9,1},{2,10},{10,2},{3,11},{11,3},{4,12},{12,4},... | collective-permute-start | bytes 1572872 | tf_op jit(solution)/shard_map/ppermute | solution.py:195
  32.7 1.9 %copy-start = (s32[4]{0:T(128)S(1)}, s32[4]{0:T(128)}, u32[]{:S(2)}) copy-start(s32[4]{0:T(128)} %lengths_ref.5) | copy-start | bytes 52
  36.9 11.6 %collective-permute-start.3 = (bf16[4,32,512]{2,1,0:T(8,128)(2,1)S(1)}, bf16[4,32,512]{2,1,0:T(8,128)(2,1)S(1)}, u32[]{:S(2)}, u32[]{:S(2)}) collective-permute-start(bf16[4,32,512]{2,1,0:T(8,128)(2,1)S(1)} %attend_sent.1), channel_id=1, source_target_pairs={{0,4},{4,0},{1,5},{5,1},{2,6},{6,2},{3,7},{7,3},{8,12},{12,8},{9,1... | collective-permute-start | bytes 393224 | tf_op jit(solution)/shard_map/ppermute | solution.py:222
  48.6 12.4 %copy-start.4 = (s32[1024]{0:T(1024)S(1)}, s32[1024]{0:T(1024)}, u32[]{:S(2)}) copy-start(s32[1024]{0:T(1024)} %slot_ref.1) | copy-start | bytes 12292
  48.6 18.2 %collective-permute-start.4 = (bf16[2,32,512]{2,1,0:T(8,128)(2,1)S(1)}, bf16[2,32,512]{2,1,0:T(8,128)(2,1)S(1)}, u32[]{:S(2)}, u32[]{:S(2)}) collective-permute-start(bf16[2,32,512]{2,1,0:T(8,128)(2,1)S(1)} %get-tuple-element.12), channel_id=1, source_target_pairs={{0,1},{1,0},{2,3},{3,2},{4,5},{5,4},{6,7},{7,6},{8,9},{9,8},{10,11... | collective-permute-start | bytes 196616 | tf_op jit(solution)/shard_map/ppermute | solution.py:233
  54.5 12.3 %collective-permute-start.5 = (bf16[2,32,512]{2,1,0:T(8,128)(2,1)S(1)}, bf16[2,32,512]{2,1,0:T(8,128)(2,1)S(1)}, u32[]{:S(2)}, u32[]{:S(2)}) collective-permute-start(bf16[2,32,512]{2,1,0:T(8,128)(2,1)S(1)} %get-tuple-element.13), channel_id=1, source_target_pairs={{0,2},{1,3},{2,0},{3,1},{4,6},{5,7},{6,4},{7,5},{8,10},{9,11},{10,... | collective-permute-start | bytes 196616 | tf_op jit(solution)/shard_map/ppermute | solution.py:233
  58.8 8.0 %collective-permute-start.6 = (bf16[2,32,512]{2,1,0:T(8,128)(2,1)S(1)}, bf16[2,32,512]{2,1,0:T(8,128)(2,1)S(1)}, u32[]{:S(2)}, u32[]{:S(2)}) collective-permute-start(bf16[2,32,512]{2,1,0:T(8,128)(2,1)S(1)} %get-tuple-element.14), channel_id=1, source_target_pairs={{0,3},{1,2},{2,1},{3,0},{4,7},{5,6},{6,5},{7,4},{8,11},{9,10},{10,... | collective-permute-start | bytes 196616 | tf_op jit(solution)/shard_map/ppermute | solution.py:233

commit v4 on v3

--- a/solution.py
+++ b/solution.py
@@ -86,7 +86,7 @@
     half, quarter = lax.axis_index("half"), lax.axis_index("quarter")
     quarters, part_rows = out_ref.shape[:2]
     rows = quarters * part_rows
-    row_start = pl.multiple_of((half if mine else 1 - half) * rows, rows)
+    block_half = half if mine else 1 - half
     pieces = [
         (own_ref, 0),
         (near_ref, 2),
@@ -94,48 +94,58 @@
         (partner_ref.at[0], jnp.where(first_core, 1, 3)),
         (partner_ref.at[1], jnp.where(first_core, 3, 1)),
     ]
-    row = row_start + lax.broadcasted_iota(jnp.int32, (rows, 1), 0)
-    column = lax.broadcasted_iota(jnp.int32, (rows, tokens), 1)
+    place = lax.broadcasted_iota(jnp.int32, (group * rows, 1), 0) % rows
+    row = (place // part_rows * HALVES + block_half) * part_rows + place % part_rows
+    column = lax.broadcasted_iota(jnp.int32, (group * rows, tokens), 1)
     first = user_first(slab * tokens + row, lengths_ref)
     causal = column <= row
     for g in range(kv_local):
         kv_columns = slice(g * HEAD_DIM, (g + 1) * HEAD_DIM)
-        for r in range(group):
-            h = g * group + r
-            query = queries_ref[pl.ds(row_start, rows), h * HEAD_DIM : (h + 1) * HEAD_DIM]
-            scores = []
-            for ref, back in pieces:
-                s = lax.dot_general(
-                    query,
-                    ref[0, :, kv_columns],
-                    (((1,), (1,)), ((), ())),
-                    preferred_element_type=jnp.float32,
-                )
-                begin = first - (slab - back) * tokens
-                if ref is far_ref:
-                    begin = jnp.maximum(begin, row + 1)
-                allowed = column >= begin
-                if ref is own_ref:
-                    allowed = allowed & causal
-                scores.append(jnp.where(allowed, s, MASKED))
-            peak = functools.reduce(jnp.maximum, scores)
-            row_max = jnp.max(peak, axis=1, keepdims=True)
-            total, mixed = None, None
-            for (ref, back), s in zip(pieces, scores):
-                shifted = jnp.exp2((s - row_max) * (QUERY_SCALE * LOG2_E))
-                part = jnp.dot(
-                    shifted.astype(jnp.bfloat16),
-                    ref[1, :, kv_columns],
-                    preferred_element_type=jnp.float32,
-                )
-                total = shifted if total is None else total + shifted
-                mixed = part if mixed is None else mixed + part
-            denominators = jnp.sum(total, axis=1, keepdims=True)
-            result = (mixed / denominators).astype(out_ref.dtype)
-            columns = slice(h * HEAD_DIM, (h + 1) * HEAD_DIM)
+        heads = range(g * group, (g + 1) * group)
+        query = jnp.concatenate(
+            [
+                queries_ref[
+                    pl.ds((target * HALVES + block_half) * part_rows, part_rows),
+                    h * HEAD_DIM : (h + 1) * HEAD_DIM,
+                ]
+                for h in heads
+                for target in range(quarters)
+            ]
+        )
+        scores = []
+        for ref, back in pieces:
+            s = lax.dot_general(
+                query,
+                ref[0, :, kv_columns],
+                (((1,), (1,)), ((), ())),
+                preferred_element_type=jnp.float32,
+            )
+            begin = first - (slab - back) * tokens
+            if ref is far_ref:
+                begin = jnp.maximum(begin, row + 1)
+            allowed = column >= begin
+            if ref is own_ref:
+                allowed = allowed & causal
+            scores.append(jnp.where(allowed, s, MASKED))
+        peak = functools.reduce(jnp.maximum, scores)
+        row_max = jnp.max(peak, axis=1, keepdims=True)
+        total, mixed = None, None
+        for (ref, back), s in zip(pieces, scores):
+            shifted = jnp.exp2((s - row_max) * (QUERY_SCALE * LOG2_E))
+            part = jnp.dot(
+                shifted.astype(jnp.bfloat16),
+                ref[1, :, kv_columns],
+                preferred_element_type=jnp.float32,
+            )
+            total = shifted if total is None else total + shifted
+            mixed = part if mixed is None else mixed + part
+        denominators = jnp.sum(total, axis=1, keepdims=True)
+        result = (mixed / denominators).astype(out_ref.dtype)
+        for r, h in enumerate(heads):
             for target in range(quarters):
-                parts_ref[target, :, columns] = result[
-                    target * part_rows : (target + 1) * part_rows
+                start = r * rows + target * part_rows
+                parts_ref[target, :, h * HEAD_DIM : (h + 1) * HEAD_DIM] = result[
+                    start : start + part_rows
                 ]
     for e in range(quarters):
         out_ref[e] = parts_ref[quarter ^ e]
@@ -154,7 +164,7 @@
     width = in_refs[0].shape[2]
     for e, ref in enumerate(in_refs):
         for half in range(HALVES):
-            start = (half * len(in_refs) + (quarter ^ e)) * width
+            start = ((quarter ^ e) * HALVES + half) * width
             out_ref[:, pl.ds(pl.multiple_of(start, width), width)] = ref[half]
 
 
@@ -263,8 +273,8 @@
     chips = mesh.shape["slab"] // CORES
     z = next(n for n in (8, 4, 2, 1) if chips % n == 0)
     x = chips // z
-    axes = ("x", "z", "core", "half", "quarter")
-    split = Mesh(mesh.devices.reshape(x, z, CORES, HALVES, y // HALVES), axes)
+    axes = ("x", "z", "core", "quarter", "half")
+    split = Mesh(mesh.devices.reshape(x, z, CORES, y // HALVES, HALVES), axes)
     slab, head = axes[:3], axes[3:]
     return jax.shard_map(
         body,

time: 67.9 us -> 64.3 us (0.947)
  starting transfers between devices: 37.2 us -> 32.9 us
  waiting for transfers between devices: 19.5 us -> 20.4 us
    ppermute x1, starting transfers between devices: 7.73 us -> 3.49 us  [body(): arrived = lax.ppermute(sent, 'half', swap)]
where the time goes in v4:
time: 64.3 us; the launch traced here: 63.6 us
  starting transfers between devices  32.9 us (51%)
  waiting for transfers between devices  20.4 us (32%)
  Pallas kernels  8.18 us (13%)
  other arithmetic  1.28 us (2%)
  between operations  0.82 us (1%)
    ppermute x3, starting transfers between devices, body(): lax.ppermute(pairs[e], 'quarter', [(i, i ^ e) for i in range(quarters)])  12.4 us
    ppermute x1, waiting for transfers between devices, body(): near = lax.ppermute(own, ('x', 'z'), forward)  11.3 us
    all_to_all x1, starting transfers between devices, body(): lax.all_to_all(outgoing, slab_axes, split_axis=0, concat_axis=0, tiled=True)  8.98 us
    ppermute x3, waiting for transfers between devices, body(): lax.ppermute(pairs[e], 'quarter', [(i, i ^ e) for i in range(quarters)])  4.87 us
    ppermute x1, starting transfers between devices, body(): near = lax.ppermute(own, ('x', 'z'), forward)  4.28 us
    pallas_call x2, Pallas kernels, body(): pl.pallas_call(functools.partial(attend_kernel, mine), out_shape=parts, i...  4.25 us
    ppermute x1, starting transfers between devices, body(): arrived = lax.ppermute(sent, 'half', swap)  3.49 us
    ppermute x1, starting transfers between devices, body(): partner = lax.ppermute(given, 'core', swap)  1.92 us
  transfers between devices with their start and end apart: 8, of which 5 were waited for; matrix products, arithmetic and copies ran while one was open for 0% of the time, Pallas kernels for 12%

profile of v4, /device:TPU:6, one launch (start us, length us, event | category | flops | bytes accessed | tf_op | source)
XLA Modules:
  0.0 63.6 jit_solution(5437457763509442207)
XLA Ops:
  0.6 1.0 %pad_maximum_fusion.1.own_ref = bf16[2,256,256]{2,1,0:T(8,128)(2,1)S(1)} fusion(bf16[1,256,256]{2,1,0:T(8,128)(2,1)} %bitcast.6, bf16[1,256,256]{2,1,0:T(8,128)(2,1)} %bitcast.8), kind=kLoop, calls=%fused_computation.1 | loop fusion | flops 131072 | bytes 524288 | tf_op jit(solution)/shard_map/stack | solution.py:184
  1.6 4.3 %collective-permute-start = (bf16[2,256,256]{2,1,0:T(8,128)(2,1)S(1)}, bf16[2,256,256]{2,1,0:T(8,128)(2,1)S(1)}, u32[]{:S(2)}, u32[]{:S(2)}) collective-permute-start(bf16[2,256,256]{2,1,0:T(8,128)(2,1)S(1)} %pad_maximum_fusion.1.own_ref), channel_id=1, source_target_pairs={{0,16},{16,32},{32,48},{48,64},{64,80},{80,96},{96,112},{112,128},... | collective-permute-start | bytes 786440 | tf_op jit(solution)/shard_map/ppermute | solution.py:199
  5.9 1.9 %prepare.1 = bf16[64,2,16,256]{3,2,1,0:T(8,128)(2,1)} custom-call(s32[4]{0:T(128)} %lengths_ref.5, s32[1024]{0:T(1024)} %slot_ref.1, bf16[256,256]{1,0:T(8,128)(2,1)} %keys_ref.1, bf16[256,256]{1,0:T(8,128)(2,1)} %values_ref.1), custom_call_target="tpu_custom_call" | custom-call | bytes 1048576 | tf_op jit(solution)/shard_map/prepare/pallas_call | solution.py:185
  7.8 11.3 %collective-permute-done.near_ref = bf16[2,256,256]{2,1,0:T(8,128)(2,1)S(1)} collective-permute-done((bf16[2,256,256]{2,1,0:T(8,128)(2,1)S(1)}, bf16[2,256,256]{2,1,0:T(8,128)(2,1)S(1)}, u32[]{:S(2)}, u32[]{:S(2)}) %collective-permute-start) | collective-permute-done | bytes 262176 | tf_op jit(solution)/shard_map/ppermute | solution.py:199
  19.1 1.9 %collective-permute-start.1 = (bf16[2,256,256]{2,1,0:T(8,128)(2,1)S(1)}, bf16[2,256,256]{2,1,0:T(8,128)(2,1)S(1)}, u32[]{:S(2)}, u32[]{:S(2)}) collective-permute-start(bf16[2,256,256]{2,1,0:T(8,128)(2,1)S(1)} %collective-permute-done.near_ref), channel_id=1, source_target_pairs={{0,16},{16,32},{32,48},{48,64},{64,80},{80,96},{96,112},{112,128},... | collective-permute-start | bytes 786440 | tf_op jit(solution)/shard_map/ppermute | solution.py:201
  21.1 0.0 copy-start.2
  21.1 0.0 copy-start.3
  21.1 9.0 %all-to-all-start = ((bf16[64,2,16,256]{3,2,1,0:T(8,128)(2,1)}), bf16[64,2,16,256]{3,2,1,0:T(8,128)(2,1)S(1)}, u32[]{:S(2)}, u32[]{:S(2)}) async-start(bf16[64,2,16,256]{3,2,1,0:T(8,128)(2,1)} %prepare.1), calls=%async_computation | async-start | bytes 2097152 | tf_op jit(solution)/shard_map/all_to_all | solution.py:202
  30.1 0.5 collective-permute-done.1.far_ref
  30.6 0.0 copy-done.2
  30.6 0.0 copy-done.3
  30.7 0.0 copy-start.1
  30.7 0.1 pad_maximum_fusion
  30.7 1.9 %collective-permute-start.2 = (bf16[2,2,256,256]{3,2,1,0:T(8,128)(2,1)S(1)}, bf16[2,2,256,256]{3,2,1,0:T(8,128)(2,1)S(1)}, u32[]{:S(2)}, u32[]{:S(2)}) collective-permute-start(bf16[2,2,256,256]{3,2,1,0:T(8,128)(2,1)S(1)} %pad_maximum_fusion), channel_id=1, source_target_pairs={{0,8},{8,0},{1,9},{9,1},{2,10},{10,2},{3,11},{11,3},{4,12},{12,4},... | collective-permute-start | bytes 1572872 | tf_op jit(solution)/shard_map/ppermute | solution.py:205
  32.7 0.0 copy-start
  32.7 1.8 %collective-permute-done.2.partner_ref = bf16[2,2,256,256]{3,2,1,0:T(8,128)(2,1)S(1)} collective-permute-done((bf16[2,2,256,256]{3,2,1,0:T(8,128)(2,1)S(1)}, bf16[2,2,256,256]{3,2,1,0:T(8,128)(2,1)S(1)}, u32[]{:S(2)}, u32[]{:S(2)}) %collective-permute-start.2) | collective-permute-done | bytes 524320 | tf_op jit(solution)/shard_map/ppermute | solution.py:205
  34.5 0.0 copy-done.1
  34.5 0.0 copy-done
  34.5 2.1 %attend_sent.1 = bf16[4,32,512]{2,1,0:T(8,128)(2,1)S(1)} custom-call(s32[4]{0:T(128)S(1)} %copy-done, bf16[256,512]{1,0:T(8,128)(2,1)S(1)} %copy-done.1, bf16[2,256,256]{2,1,0:T(8,128)(2,1)S(1)} %pad_maximum_fusion.1.own_ref, bf16[2,256,256]{2,1,0:T(8,128)(2,1)S(1)} %collective-permute-done.near_ref, ...), custom_call_target="tpu_custom_call" | custom-call | flops 5704253440 | bytes 2097152 | tf_op jit(solution)/shard_map/attend_sent/pallas_call | solution.py:218
  36.7 3.5 %collective-permute-start.3 = (bf16[4,32,512]{2,1,0:T(8,128)(2,1)S(1)}, bf16[4,32,512]{2,1,0:T(8,128)(2,1)S(1)}, u32[]{:S(2)}, u32[]{:S(2)}) collective-permute-start(bf16[4,32,512]{2,1,0:T(8,128)(2,1)S(1)} %attend_sent.1), channel_id=1, source_target_pairs={{0,1},{1,0},{2,3},{3,2},{4,5},{5,4},{6,7},{7,6},{8,9},{9,8},{10,11... | collective-permute-start | bytes 393224 | tf_op jit(solution)/shard_map/ppermute | solution.py:232
  40.2 2.1 %attend_kept.1.kept_ref = bf16[4,32,512]{2,1,0:T(8,128)(2,1)S(1)} custom-call(s32[4]{0:T(128)S(1)} %copy-done, bf16[256,512]{1,0:T(8,128)(2,1)S(1)} %copy-done.1, bf16[2,256,256]{2,1,0:T(8,128)(2,1)S(1)} %pad_maximum_fusion.1.own_ref, bf16[2,256,256]{2,1,0:T(8,128)(2,1)S(1)} %collective-permute-done.near_ref, ...), custom_call_target="tpu_custom_call" | custom-call | flops 5704253440 | bytes 2097152 | tf_op jit(solution)/shard_map/attend_kept/pallas_call | solution.py:218
  42.3 1.8 %collective-permute-done.3.arrived_ref = bf16[4,32,512]{2,1,0:T(8,128)(2,1)S(1)} collective-permute-done((bf16[4,32,512]{2,1,0:T(8,128)(2,1)S(1)}, bf16[4,32,512]{2,1,0:T(8,128)(2,1)S(1)}, u32[]{:S(2)}, u32[]{:S(2)}) %collective-permute-start.3) | collective-permute-done | bytes 131104 | tf_op jit(solution)/shard_map/ppermute | solution.py:232
  44.1 0.0 copy-start.4
  44.1 4.5 %collective-permute-start.4 = (bf16[2,32,512]{2,1,0:T(8,128)(2,1)S(1)}, bf16[2,32,512]{2,1,0:T(8,128)(2,1)S(1)}, u32[]{:S(2)}, u32[]{:S(2)}) collective-permute-start(bf16[2,32,512]{2,1,0:T(8,128)(2,1)S(1)} %get-tuple-element.12), channel_id=1, source_target_pairs={{0,2},{2,0},{4,6},{6,4},{1,3},{3,1},{5,7},{7,5},{8,10},{10,8},{12,... | collective-permute-start | bytes 196616 | tf_op jit(solution)/shard_map/ppermute | solution.py:243
  48.7 5.9 %collective-permute-start.5 = (bf16[2,32,512]{2,1,0:T(8,128)(2,1)S(1)}, bf16[2,32,512]{2,1,0:T(8,128)(2,1)S(1)}, u32[]{:S(2)}, u32[]{:S(2)}) collective-permute-start(bf16[2,32,512]{2,1,0:T(8,128)(2,1)S(1)} %get-tuple-element.13), channel_id=1, source_target_pairs={{0,4},{2,6},{4,0},{6,2},{1,5},{3,7},{5,1},{7,3},{8,12},{10,14},{12... | collective-permute-start | bytes 196616 | tf_op jit(solution)/shard_map/ppermute | solution.py:243
  54.6 1.9 %collective-permute-start.6 = (bf16[2,32,512]{2,1,0:T(8,128)(2,1)S(1)}, bf16[2,32,512]{2,1,0:T(8,128)(2,1)S(1)}, u32[]{:S(2)}, u32[]{:S(2)}) collective-permute-start(bf16[2,32,512]{2,1,0:T(8,128)(2,1)S(1)} %get-tuple-element.14), channel_id=1, source_target_pairs={{0,6},{2,4},{4,2},{6,0},{1,7},{3,5},{5,3},{7,1},{8,14},{10,12},{12... | collective-permute-start | bytes 196616 | tf_op jit(solution)/shard_map/ppermute | solution.py:243
  56.5 0.0 copy-done.4
  56.5 0.2 select_reduce_fusion.source_ref
  56.7 0.0 all-to-all-done.in_ref
  56.7 1.3 %collect.1 = bf16[16,2,16,256]{3,2,1,0:T(8,128)(2,1)} custom-call(s32[16]{0:T(128)S(1)} %select_reduce_fusion.source_ref, bf16[64,2,16,256]{3,2,1,0:T(8,128)(2,1)S(1)} %all-to-all-done.in_ref), custom_call_target="tpu_custom_call" | custom-call | bytes 524288 | tf_op jit(solution)/shard_map/collect/pallas_call | solution.py:246
  58.0 4.9 %collective-permute-done.6.refs_3_ = bf16[2,32,512]{2,1,0:T(8,128)(2,1)S(1)} collective-permute-done((bf16[2,32,512]{2,1,0:T(8,128)(2,1)S(1)}, bf16[2,32,512]{2,1,0:T(8,128)(2,1)S(1)}, u32[]{:S(2)}, u32[]{:S(2)}) %collective-permute-start.6) | collective-permute-done | bytes 65568 | tf_op jit(solution)/shard_map/ppermute | solution.py:243
  62.9 0.0 collective-permute-done.4.refs_1_
  62.9 0.0 collective-permute-done.5.refs_2_
  62.9 0.7 %join.1 = bf16[32,4096]{1,0:T(8,128)(2,1)} custom-call(bf16[2,32,512]{2,1,0:T(8,128)(2,1)S(1)} %get-tuple-element.11.refs_0_, bf16[2,32,512]{2,1,0:T(8,128)(2,1)S(1)} %collective-permute-done.4.refs_1_, bf16[2,32,512]{2,1,0:T(8,128)(2,1)S(1)} %collective-permute-done.5.refs_2_, bf16[2,32,512]{2,1,0:T(8,128)(2,1)S(1)} %collective-permute-done.6.refs_3_), custom_call_target="tpu_custom_call" | custom-call | bytes 524288 | tf_op jit(solution)/shard_map/join/pallas_call | solution.py:256
  (4 shorter events, 0.1 us)
Async XLA Ops:
  1.6 17.5 %collective-permute-start = (bf16[2,256,256]{2,1,0:T(8,128)(2,1)S(1)}, bf16[2,256,256]{2,1,0:T(8,128)(2,1)S(1)}, u32[]{:S(2)}, u32[]{:S(2)}) collective-permute-start(bf16[2,256,256]{2,1,0:T(8,128)(2,1)S(1)} %pad_maximum_fusion.1.own_ref), channel_id=1, source_target_pairs={{0,16},{16,32},{32,48},{48,64},{64,80},{80,96},{96,112},{112,128},... | collective-permute-start | bytes 786440 | tf_op jit(solution)/shard_map/ppermute | solution.py:199
  19.1 11.5 %collective-permute-start.1 = (bf16[2,256,256]{2,1,0:T(8,128)(2,1)S(1)}, bf16[2,256,256]{2,1,0:T(8,128)(2,1)S(1)}, u32[]{:S(2)}, u32[]{:S(2)}) collective-permute-start(bf16[2,256,256]{2,1,0:T(8,128)(2,1)S(1)} %collective-permute-done.near_ref), channel_id=1, source_target_pairs={{0,16},{16,32},{32,48},{48,64},{64,80},{80,96},{96,112},{112,128},... | collective-permute-start | bytes 786440 | tf_op jit(solution)/shard_map/ppermute | solution.py:201
  21.1 9.6 %copy-start.2 = (bf16[256,256]{1,0:T(8,128)(2,1)S(1)}, bf16[256,256]{1,0:T(8,128)(2,1)}, u32[]{:S(2)}) copy-start(bf16[256,256]{1,0:T(8,128)(2,1)} %values_ref.1) | copy-start | bytes 393220
  21.1 9.6 %copy-start.3 = (bf16[256,256]{1,0:T(8,128)(2,1)S(1)}, bf16[256,256]{1,0:T(8,128)(2,1)}, u32[]{:S(2)}) copy-start(bf16[256,256]{1,0:T(8,128)(2,1)} %keys_ref.1) | copy-start | bytes 393220
  21.1 35.6 %all-to-all-start = ((bf16[64,2,16,256]{3,2,1,0:T(8,128)(2,1)}), bf16[64,2,16,256]{3,2,1,0:T(8,128)(2,1)S(1)}, u32[]{:S(2)}, u32[]{:S(2)}) async-start(bf16[64,2,16,256]{3,2,1,0:T(8,128)(2,1)} %prepare.1), calls=%async_computation | async-start | bytes 2097152 | tf_op jit(solution)/shard_map/all_to_all | solution.py:202
  30.7 3.9 %copy-start.1 = (bf16[256,512]{1,0:T(8,128)(2,1)S(1)}, bf16[256,512]{1,0:T(8,128)(2,1)}, u32[]{:S(2)}) copy-start(bf16[256,512]{1,0:T(8,128)(2,1)} %queries_ref.3) | copy-start | bytes 786436
  30.7 3.8 %collective-permute-start.2 = (bf16[2,2,256,256]{3,2,1,0:T(8,128)(2,1)S(1)}, bf16[2,2,256,256]{3,2,1,0:T(8,128)(2,1)S(1)}, u32[]{:S(2)}, u32[]{:S(2)}) collective-permute-start(bf16[2,2,256,256]{3,2,1,0:T(8,128)(2,1)S(1)} %pad_maximum_fusion), channel_id=1, source_target_pairs={{0,8},{8,0},{1,9},{9,1},{2,10},{10,2},{3,11},{11,3},{4,12},{12,4},... | collective-permute-start | bytes 1572872 | tf_op jit(solution)/shard_map/ppermute | solution.py:205
  32.7 1.9 %copy-start = (s32[4]{0:T(128)S(1)}, s32[4]{0:T(128)}, u32[]{:S(2)}) copy-start(s32[4]{0:T(128)} %lengths_ref.5) | copy-start | bytes 52
  36.7 7.4 %collective-permute-start.3 = (bf16[4,32,512]{2,1,0:T(8,128)(2,1)S(1)}, bf16[4,32,512]{2,1,0:T(8,128)(2,1)S(1)}, u32[]{:S(2)}, u32[]{:S(2)}) collective-permute-start(bf16[4,32,512]{2,1,0:T(8,128)(2,1)S(1)} %attend_sent.1), channel_id=1, source_target_pairs={{0,1},{1,0},{2,3},{3,2},{4,5},{5,4},{6,7},{7,6},{8,9},{9,8},{10,11... | collective-permute-start | bytes 393224 | tf_op jit(solution)/shard_map/ppermute | solution.py:232
  44.1 12.4 %copy-start.4 = (s32[1024]{0:T(1024)S(1)}, s32[1024]{0:T(1024)}, u32[]{:S(2)}) copy-start(s32[1024]{0:T(1024)} %slot_ref.1) | copy-start | bytes 12292
  44.1 18.7 %collective-permute-start.4 = (bf16[2,32,512]{2,1,0:T(8,128)(2,1)S(1)}, bf16[2,32,512]{2,1,0:T(8,128)(2,1)S(1)}, u32[]{:S(2)}, u32[]{:S(2)}) collective-permute-start(bf16[2,32,512]{2,1,0:T(8,128)(2,1)S(1)} %get-tuple-element.12), channel_id=1, source_target_pairs={{0,2},{2,0},{4,6},{6,4},{1,3},{3,1},{5,7},{7,5},{8,10},{10,8},{12,... | collective-permute-start | bytes 196616 | tf_op jit(solution)/shard_map/ppermute | solution.py:243
  48.7 14.2 %collective-permute-start.5 = (bf16[2,32,512]{2,1,0:T(8,128)(2,1)S(1)}, bf16[2,32,512]{2,1,0:T(8,128)(2,1)S(1)}, u32[]{:S(2)}, u32[]{:S(2)}) collective-permute-start(bf16[2,32,512]{2,1,0:T(8,128)(2,1)S(1)} %get-tuple-element.13), channel_id=1, source_target_pairs={{0,4},{2,6},{4,0},{6,2},{1,5},{3,7},{5,1},{7,3},{8,12},{10,14},{12... | collective-permute-start | bytes 196616 | tf_op jit(solution)/shard_map/ppermute | solution.py:243
  54.6 8.3 %collective-permute-start.6 = (bf16[2,32,512]{2,1,0:T(8,128)(2,1)S(1)}, bf16[2,32,512]{2,1,0:T(8,128)(2,1)S(1)}, u32[]{:S(2)}, u32[]{:S(2)}) collective-permute-start(bf16[2,32,512]{2,1,0:T(8,128)(2,1)S(1)} %get-tuple-element.14), channel_id=1, source_target_pairs={{0,6},{2,4},{4,2},{6,0},{1,7},{3,5},{5,3},{7,1},{8,14},{10,12},{12... | collective-permute-start | bytes 196616 | tf_op jit(solution)/shard_map/ppermute | solution.py:243

commit v5 on v4

--- a/solution.py
+++ b/solution.py
@@ -48,6 +48,17 @@
     core = lax.axis_index("core")
     chip = lax.axis_index("x") * lax.axis_size("z") + lax.axis_index("z")
     return chip * CORES + core, core
+
+
+def stack_kernel(keys_ref, values_ref, own_ref, sems):
+    copies = [
+        pltpu.make_async_copy(ref, own_ref.at[side], sems.at[side])
+        for side, ref in enumerate((keys_ref, values_ref))
+    ]
+    for copy in copies:
+        copy.start()
+    for copy in copies:
+        copy.wait()
 
 
 def prepare_kernel(lengths_ref, slot_ref, keys_ref, values_ref, out_ref, live_ref, sems):
@@ -181,7 +192,16 @@
     core = lax.axis_index("core")
 
     page_block = (2, PAGE_ROWS, kv_width)
-    own = jnp.stack([keys, values])
+    own = pl.pallas_call(
+        stack_kernel,
+        out_shape=jax.ShapeDtypeStruct((2, tokens, kv_width), jnp.bfloat16),
+        in_specs=[ANY, ANY],
+        out_specs=VMEM,
+        scratch_shapes=[pltpu.SemaphoreType.DMA((2,))],
+        cost_estimate=cost(0, tokens * kv_width * 8),
+        compiler_params=pltpu.CompilerParams(vmem_limit_bytes=4 << 20),
+        name="stack",
+    )(keys, values)
     outgoing = pl.pallas_call(
         prepare_kernel,
         out_shape=jax.ShapeDtypeStruct((slabs,) + page_block, jnp.bfloat16),

time: 64.3 us -> 65.4 us (1.017)
  local copies, waits for them, and re-layouts: 0.03 us -> 1.82 us
  other arithmetic: 1.28 us -> 0.28 us
    unnamed x10, local copies, waits for them, and re-layouts: 0.03 us -> 1.82 us
    another operation x1 -> x0, other arithmetic: 1 us -> none  [body(): own = jnp.stack([keys, values])]
  transfers between devices with their start and end apart: 8 -> 8, of which waited for: 5 -> 5; matrix products, arithmetic and copies ran while one was open for 0% -> 0% of each run, Pallas kernels for 12% -> 11%
where the time goes in v5:
time: 65.4 us; the launch traced here: 64.7 us
  starting transfers between devices  32.8 us (50%)
  waiting for transfers between devices  20.5 us (31%)
  Pallas kernels  8.48 us (13%)
  local copies, waits for them, and re-layouts  1.82 us (3%)
  between operations  0.82 us (1%)
    ppermute x3, starting transfers between devices, body(): lax.ppermute(pairs[e], 'quarter', [(i, i ^ e) for i in range(quarters)])  12.4 us
    ppermute x1, waiting for transfers between devices, body(): near = lax.ppermute(own, ('x', 'z'), forward)  11.3 us
    all_to_all x1, starting transfers between devices, body(): lax.all_to_all(outgoing, slab_axes, split_axis=0, concat_axis=0, tiled=True)  8.85 us
    ppermute x3, waiting for transfers between devices, body(): lax.ppermute(pairs[e], 'quarter', [(i, i ^ e) for i in range(quarters)])  4.87 us
    ppermute x1, starting transfers between devices, body(): near = lax.ppermute(own, ('x', 'z'), forward)  4.28 us
    pallas_call x2, Pallas kernels, body(): pl.pallas_call(functools.partial(attend_kernel, mine), out_shape=parts, i...  4.24 us
    ppermute x1, starting transfers between devices, body(): arrived = lax.ppermute(sent, 'half', swap)  3.48 us
    ppermute x1, starting transfers between devices, body(): partner = lax.ppermute(given, 'core', swap)  1.92 us
  transfers between devices with their start and end apart: 8, of which 5 were waited for; matrix products, arithmetic and copies ran while one was open for 0% of the time, Pallas kernels for 11%

profile of v5, /device:TPU:6, one launch (start us, length us, event | category | flops | bytes accessed | tf_op | source)
XLA Modules:
  0.0 64.7 jit_solution(13702045000884188148)
XLA Ops:
  0.6 0.0 copy-start
  0.6 0.9 %copy-done = bf16[256,256]{1,0:T(8,128)(2,1)S(1)} copy-done((bf16[256,256]{1,0:T(8,128)(2,1)S(1)}, bf16[256,256]{1,0:T(8,128)(2,1)}, u32[]{:S(2)}) %copy-start) | copy-done | bytes 131096
  1.5 0.0 copy-start.1
  1.5 0.9 %copy-done.1 = bf16[256,256]{1,0:T(8,128)(2,1)S(1)} copy-done((bf16[256,256]{1,0:T(8,128)(2,1)S(1)}, bf16[256,256]{1,0:T(8,128)(2,1)}, u32[]{:S(2)}) %copy-start.1) | copy-done | bytes 131096
  2.4 0.3 stack.13.own_ref
  2.8 4.3 %collective-permute-start = (bf16[2,256,256]{2,1,0:T(8,128)(2,1)S(1)}, bf16[2,256,256]{2,1,0:T(8,128)(2,1)S(1)}, u32[]{:S(2)}, u32[]{:S(2)}) collective-permute-start(bf16[2,256,256]{2,1,0:T(8,128)(2,1)S(1)} %stack.13.own_ref), channel_id=1, source_target_pairs={{0,16},{16,32},{32,48},{48,64},{64,80},{80,96},{96,112},{112,128},... | collective-permute-start | bytes 786440 | tf_op jit(solution)/shard_map/ppermute | solution.py:219
  7.1 1.9 %prepare.1 = bf16[64,2,16,256]{3,2,1,0:T(8,128)(2,1)} custom-call(s32[4]{0:T(128)} %lengths_ref.5, s32[1024]{0:T(1024)} %slot_ref.1, bf16[256,256]{1,0:T(8,128)(2,1)} %keys_ref.3, bf16[256,256]{1,0:T(8,128)(2,1)} %values_ref.3), custom_call_target="tpu_custom_call" | custom-call | bytes 1048576 | tf_op jit(solution)/shard_map/prepare/pallas_call | solution.py:205
  9.0 11.3 %collective-permute-done.near_ref = bf16[2,256,256]{2,1,0:T(8,128)(2,1)S(1)} collective-permute-done((bf16[2,256,256]{2,1,0:T(8,128)(2,1)S(1)}, bf16[2,256,256]{2,1,0:T(8,128)(2,1)S(1)}, u32[]{:S(2)}, u32[]{:S(2)}) %collective-permute-start) | collective-permute-done | bytes 262176 | tf_op jit(solution)/shard_map/ppermute | solution.py:219
  20.3 1.9 %collective-permute-start.1 = (bf16[2,256,256]{2,1,0:T(8,128)(2,1)S(1)}, bf16[2,256,256]{2,1,0:T(8,128)(2,1)S(1)}, u32[]{:S(2)}, u32[]{:S(2)}) collective-permute-start(bf16[2,256,256]{2,1,0:T(8,128)(2,1)S(1)} %collective-permute-done.near_ref), channel_id=1, source_target_pairs={{0,16},{16,32},{32,48},{48,64},{64,80},{80,96},{96,112},{112,128},... | collective-permute-start | bytes 786440 | tf_op jit(solution)/shard_map/ppermute | solution.py:221
  22.2 8.8 %all-to-all-start = ((bf16[64,2,16,256]{3,2,1,0:T(8,128)(2,1)}), bf16[64,2,16,256]{3,2,1,0:T(8,128)(2,1)S(1)}, u32[]{:S(2)}, u32[]{:S(2)}) async-start(bf16[64,2,16,256]{3,2,1,0:T(8,128)(2,1)} %prepare.1), calls=%async_computation | async-start | bytes 2097152 | tf_op jit(solution)/shard_map/all_to_all | solution.py:222
  31.1 0.7 %collective-permute-done.1.far_ref = bf16[2,256,256]{2,1,0:T(8,128)(2,1)S(1)} collective-permute-done((bf16[2,256,256]{2,1,0:T(8,128)(2,1)S(1)}, bf16[2,256,256]{2,1,0:T(8,128)(2,1)S(1)}, u32[]{:S(2)}, u32[]{:S(2)}) %collective-permute-start.1) | collective-permute-done | bytes 262176 | tf_op jit(solution)/shard_map/ppermute | solution.py:221
  31.8 0.0 copy-start.3
  31.8 0.1 pad_maximum_fusion
  31.9 1.9 %collective-permute-start.2 = (bf16[2,2,256,256]{3,2,1,0:T(8,128)(2,1)S(1)}, bf16[2,2,256,256]{3,2,1,0:T(8,128)(2,1)S(1)}, u32[]{:S(2)}, u32[]{:S(2)}) collective-permute-start(bf16[2,2,256,256]{3,2,1,0:T(8,128)(2,1)S(1)} %pad_maximum_fusion), channel_id=1, source_target_pairs={{0,8},{8,0},{1,9},{9,1},{2,10},{10,2},{3,11},{11,3},{4,12},{12,4},... | collective-permute-start | bytes 1572872 | tf_op jit(solution)/shard_map/ppermute | solution.py:225
  33.8 0.0 copy-start.2
  33.8 1.8 %collective-permute-done.2.partner_ref = bf16[2,2,256,256]{3,2,1,0:T(8,128)(2,1)S(1)} collective-permute-done((bf16[2,2,256,256]{3,2,1,0:T(8,128)(2,1)S(1)}, bf16[2,2,256,256]{3,2,1,0:T(8,128)(2,1)S(1)}, u32[]{:S(2)}, u32[]{:S(2)}) %collective-permute-start.2) | collective-permute-done | bytes 524320 | tf_op jit(solution)/shard_map/ppermute | solution.py:225
  35.7 0.0 copy-done.3
  35.7 0.0 copy-done.2
  35.7 2.1 %attend_sent.1 = bf16[4,32,512]{2,1,0:T(8,128)(2,1)S(1)} custom-call(s32[4]{0:T(128)S(1)} %copy-done.2, bf16[256,512]{1,0:T(8,128)(2,1)S(1)} %copy-done.3, bf16[2,256,256]{2,1,0:T(8,128)(2,1)S(1)} %stack.13.own_ref, bf16[2,256,256]{2,1,0:T(8,128)(2,1)S(1)} %collective-permute-done.near_ref, bf16[2,256,256]{2,1,0:T(8,128)(2,1)S(1)} %collective-permute-done.1.far_ref, ...), custom_call_target="tpu_custom_call" | custom-call | flops 5704253440 | bytes 2097152 | tf_op jit(solution)/shard_map/attend_sent/pallas_call | solution.py:238
  37.8 3.5 %collective-permute-start.3 = (bf16[4,32,512]{2,1,0:T(8,128)(2,1)S(1)}, bf16[4,32,512]{2,1,0:T(8,128)(2,1)S(1)}, u32[]{:S(2)}, u32[]{:S(2)}) collective-permute-start(bf16[4,32,512]{2,1,0:T(8,128)(2,1)S(1)} %attend_sent.1), channel_id=1, source_target_pairs={{0,1},{1,0},{2,3},{3,2},{4,5},{5,4},{6,7},{7,6},{8,9},{9,8},{10,11... | collective-permute-start | bytes 393224 | tf_op jit(solution)/shard_map/ppermute | solution.py:252
  41.3 2.1 %attend_kept.1.kept_ref = bf16[4,32,512]{2,1,0:T(8,128)(2,1)S(1)} custom-call(s32[4]{0:T(128)S(1)} %copy-done.2, bf16[256,512]{1,0:T(8,128)(2,1)S(1)} %copy-done.3, bf16[2,256,256]{2,1,0:T(8,128)(2,1)S(1)} %stack.13.own_ref, bf16[2,256,256]{2,1,0:T(8,128)(2,1)S(1)} %collective-permute-done.near_ref, bf16[2,256,256]{2,1,0:T(8,128)(2,1)S(1)} %collective-permute-done.1.far_ref, ...), custom_call_target="tpu_custom_call" | custom-call | flops 5704253440 | bytes 2097152 | tf_op jit(solution)/shard_map/attend_kept/pallas_call | solution.py:238
  43.4 1.8 %collective-permute-done.3.arrived_ref = bf16[4,32,512]{2,1,0:T(8,128)(2,1)S(1)} collective-permute-done((bf16[4,32,512]{2,1,0:T(8,128)(2,1)S(1)}, bf16[4,32,512]{2,1,0:T(8,128)(2,1)S(1)}, u32[]{:S(2)}, u32[]{:S(2)}) %collective-permute-start.3) | collective-permute-done | bytes 131104 | tf_op jit(solution)/shard_map/ppermute | solution.py:252
  45.3 0.0 copy-start.4
  45.3 4.5 %collective-permute-start.4 = (bf16[2,32,512]{2,1,0:T(8,128)(2,1)S(1)}, bf16[2,32,512]{2,1,0:T(8,128)(2,1)S(1)}, u32[]{:S(2)}, u32[]{:S(2)}) collective-permute-start(bf16[2,32,512]{2,1,0:T(8,128)(2,1)S(1)} %get-tuple-element.12), channel_id=1, source_target_pairs={{0,2},{2,0},{4,6},{6,4},{1,3},{3,1},{5,7},{7,5},{8,10},{10,8},{12,... | collective-permute-start | bytes 196616 | tf_op jit(solution)/shard_map/ppermute | solution.py:263
  49.8 5.9 %collective-permute-start.5 = (bf16[2,32,512]{2,1,0:T(8,128)(2,1)S(1)}, bf16[2,32,512]{2,1,0:T(8,128)(2,1)S(1)}, u32[]{:S(2)}, u32[]{:S(2)}) collective-permute-start(bf16[2,32,512]{2,1,0:T(8,128)(2,1)S(1)} %get-tuple-element.13), channel_id=1, source_target_pairs={{0,4},{2,6},{4,0},{6,2},{1,5},{3,7},{5,1},{7,3},{8,12},{10,14},{12... | collective-permute-start | bytes 196616 | tf_op jit(solution)/shard_map/ppermute | solution.py:263
  55.7 1.9 %collective-permute-start.6 = (bf16[2,32,512]{2,1,0:T(8,128)(2,1)S(1)}, bf16[2,32,512]{2,1,0:T(8,128)(2,1)S(1)}, u32[]{:S(2)}, u32[]{:S(2)}) collective-permute-start(bf16[2,32,512]{2,1,0:T(8,128)(2,1)S(1)} %get-tuple-element.14), channel_id=1, source_target_pairs={{0,6},{2,4},{4,2},{6,0},{1,7},{3,5},{5,3},{7,1},{8,14},{10,12},{12... | collective-permute-start | bytes 196616 | tf_op jit(solution)/shard_map/ppermute | solution.py:263
  57.7 0.0 copy-done.4
  57.7 0.2 select_reduce_fusion.source_ref
  57.9 0.0 all-to-all-done.in_ref
  57.9 1.3 %collect.1 = bf16[16,2,16,256]{3,2,1,0:T(8,128)(2,1)} custom-call(s32[16]{0:T(128)S(1)} %select_reduce_fusion.source_ref, bf16[64,2,16,256]{3,2,1,0:T(8,128)(2,1)S(1)} %all-to-all-done.in_ref), custom_call_target="tpu_custom_call" | custom-call | bytes 524288 | tf_op jit(solution)/shard_map/collect/pallas_call | solution.py:266
  59.1 4.9 %collective-permute-done.6.refs_3_ = bf16[2,32,512]{2,1,0:T(8,128)(2,1)S(1)} collective-permute-done((bf16[2,32,512]{2,1,0:T(8,128)(2,1)S(1)}, bf16[2,32,512]{2,1,0:T(8,128)(2,1)S(1)}, u32[]{:S(2)}, u32[]{:S(2)}) %collective-permute-start.6) | collective-permute-done | bytes 65568 | tf_op jit(solution)/shard_map/ppermute | solution.py:263
  64.0 0.0 collective-permute-done.4.refs_1_
  64.0 0.0 collective-permute-done.5.refs_2_
  64.0 0.7 %join.1 = bf16[32,4096]{1,0:T(8,128)(2,1)} custom-call(bf16[2,32,512]{2,1,0:T(8,128)(2,1)S(1)} %get-tuple-element.11.refs_0_, bf16[2,32,512]{2,1,0:T(8,128)(2,1)S(1)} %collective-permute-done.4.refs_1_, bf16[2,32,512]{2,1,0:T(8,128)(2,1)S(1)} %collective-permute-done.5.refs_2_, bf16[2,32,512]{2,1,0:T(8,128)(2,1)S(1)} %collective-permute-done.6.refs_3_), custom_call_target="tpu_custom_call" | custom-call | bytes 524288 | tf_op jit(solution)/shard_map/join/pallas_call | solution.py:276
  (4 shorter events, 0.1 us)
Async XLA Ops:
  0.6 0.9 %copy-start = (bf16[256,256]{1,0:T(8,128)(2,1)S(1)}, bf16[256,256]{1,0:T(8,128)(2,1)}, u32[]{:S(2)}) copy-start(bf16[256,256]{1,0:T(8,128)(2,1)} %keys_ref.3) | copy-start | bytes 393220
  1.5 0.9 %copy-start.1 = (bf16[256,256]{1,0:T(8,128)(2,1)S(1)}, bf16[256,256]{1,0:T(8,128)(2,1)}, u32[]{:S(2)}) copy-start(bf16[256,256]{1,0:T(8,128)(2,1)} %values_ref.3) | copy-start | bytes 393220
  2.8 17.5 %collective-permute-start = (bf16[2,256,256]{2,1,0:T(8,128)(2,1)S(1)}, bf16[2,256,256]{2,1,0:T(8,128)(2,1)S(1)}, u32[]{:S(2)}, u32[]{:S(2)}) collective-permute-start(bf16[2,256,256]{2,1,0:T(8,128)(2,1)S(1)} %stack.13.own_ref), channel_id=1, source_target_pairs={{0,16},{16,32},{32,48},{48,64},{64,80},{80,96},{96,112},{112,128},... | collective-permute-start | bytes 786440 | tf_op jit(solution)/shard_map/ppermute | solution.py:219
  20.3 11.5 %collective-permute-start.1 = (bf16[2,256,256]{2,1,0:T(8,128)(2,1)S(1)}, bf16[2,256,256]{2,1,0:T(8,128)(2,1)S(1)}, u32[]{:S(2)}, u32[]{:S(2)}) collective-permute-start(bf16[2,256,256]{2,1,0:T(8,128)(2,1)S(1)} %collective-permute-done.near_ref), channel_id=1, source_target_pairs={{0,16},{16,32},{32,48},{48,64},{64,80},{80,96},{96,112},{112,128},... | collective-permute-start | bytes 786440 | tf_op jit(solution)/shard_map/ppermute | solution.py:221
  22.2 35.7 %all-to-all-start = ((bf16[64,2,16,256]{3,2,1,0:T(8,128)(2,1)}), bf16[64,2,16,256]{3,2,1,0:T(8,128)(2,1)S(1)}, u32[]{:S(2)}, u32[]{:S(2)}) async-start(bf16[64,2,16,256]{3,2,1,0:T(8,128)(2,1)} %prepare.1), calls=%async_computation | async-start | bytes 2097152 | tf_op jit(solution)/shard_map/all_to_all | solution.py:222
  31.8 3.9 %copy-start.3 = (bf16[256,512]{1,0:T(8,128)(2,1)S(1)}, bf16[256,512]{1,0:T(8,128)(2,1)}, u32[]{:S(2)}) copy-start(bf16[256,512]{1,0:T(8,128)(2,1)} %queries_ref.3) | copy-start | bytes 786436
  31.9 3.8 %collective-permute-start.2 = (bf16[2,2,256,256]{3,2,1,0:T(8,128)(2,1)S(1)}, bf16[2,2,256,256]{3,2,1,0:T(8,128)(2,1)S(1)}, u32[]{:S(2)}, u32[]{:S(2)}) collective-permute-start(bf16[2,2,256,256]{3,2,1,0:T(8,128)(2,1)S(1)} %pad_maximum_fusion), channel_id=1, source_target_pairs={{0,8},{8,0},{1,9},{9,1},{2,10},{10,2},{3,11},{11,3},{4,12},{12,4},... | collective-permute-start | bytes 1572872 | tf_op jit(solution)/shard_map/ppermute | solution.py:225
  33.8 1.9 %copy-start.2 = (s32[4]{0:T(128)S(1)}, s32[4]{0:T(128)}, u32[]{:S(2)}) copy-start(s32[4]{0:T(128)} %lengths_ref.5) | copy-start | bytes 52
  37.8 7.4 %collective-permute-start.3 = (bf16[4,32,512]{2,1,0:T(8,128)(2,1)S(1)}, bf16[4,32,512]{2,1,0:T(8,128)(2,1)S(1)}, u32[]{:S(2)}, u32[]{:S(2)}) collective-permute-start(bf16[4,32,512]{2,1,0:T(8,128)(2,1)S(1)} %attend_sent.1), channel_id=1, source_target_pairs={{0,1},{1,0},{2,3},{3,2},{4,5},{5,4},{6,7},{7,6},{8,9},{9,8},{10,11... | collective-permute-start | bytes 393224 | tf_op jit(solution)/shard_map/ppermute | solution.py:252
  45.3 12.4 %copy-start.4 = (s32[1024]{0:T(1024)S(1)}, s32[1024]{0:T(1024)}, u32[]{:S(2)}) copy-start(s32[1024]{0:T(1024)} %slot_ref.1) | copy-start | bytes 12292
  45.3 18.7 %collective-permute-start.4 = (bf16[2,32,512]{2,1,0:T(8,128)(2,1)S(1)}, bf16[2,32,512]{2,1,0:T(8,128)(2,1)S(1)}, u32[]{:S(2)}, u32[]{:S(2)}) collective-permute-start(bf16[2,32,512]{2,1,0:T(8,128)(2,1)S(1)} %get-tuple-element.12), channel_id=1, source_target_pairs={{0,2},{2,0},{4,6},{6,4},{1,3},{3,1},{5,7},{7,5},{8,10},{10,8},{12,... | collective-permute-start | bytes 196616 | tf_op jit(solution)/shard_map/ppermute | solution.py:263
  49.8 14.2 %collective-permute-start.5 = (bf16[2,32,512]{2,1,0:T(8,128)(2,1)S(1)}, bf16[2,32,512]{2,1,0:T(8,128)(2,1)S(1)}, u32[]{:S(2)}, u32[]{:S(2)}) collective-permute-start(bf16[2,32,512]{2,1,0:T(8,128)(2,1)S(1)} %get-tuple-element.13), channel_id=1, source_target_pairs={{0,4},{2,6},{4,0},{6,2},{1,5},{3,7},{5,1},{7,3},{8,12},{10,14},{12... | collective-permute-start | bytes 196616 | tf_op jit(solution)/shard_map/ppermute | solution.py:263
  55.7 8.3 %collective-permute-start.6 = (bf16[2,32,512]{2,1,0:T(8,128)(2,1)S(1)}, bf16[2,32,512]{2,1,0:T(8,128)(2,1)S(1)}, u32[]{:S(2)}, u32[]{:S(2)}) collective-permute-start(bf16[2,32,512]{2,1,0:T(8,128)(2,1)S(1)} %get-tuple-element.14), channel_id=1, source_target_pairs={{0,6},{2,4},{4,2},{6,0},{1,7},{3,5},{5,3},{7,1},{8,14},{10,12},{12... | collective-permute-start | bytes 196616 | tf_op jit(solution)/shard_map/ppermute | solution.py:263
